TPU v7x, 32 devices: a whole 2x2x4 slice. The times are simulated.
32 devices in a mesh: dp: 4 (over y, x), expert: 8 (over z, core).
Axes of the slice: x: 2, y: 2, z: 4, core: 2. Of those that a mesh axis runs over, the one named last changes fastest.
Arguments:
- tokens: bfloat16 [4, 1024, 1280], P('dp', 'expert'), may hold values from -6 to 6
- cotangent: bfloat16 [4, 1024, 1280], P('dp', 'expert'), may hold values from -6 to 6
- attn_gain: bfloat16 [1280], P('expert'), may hold values from 0.099609375 to 1.8984375
- ffn_gain: bfloat16 [1280], P('expert'), may hold values from 0.099609375 to 1.8984375
- w_query: bfloat16 [1280, 1280], P('expert'), may hold values from -0.15625 to 0.15625
- w_key: bfloat16 [1280, 1280], P('expert'), may hold values from -0.15625 to 0.15625
- w_value: bfloat16 [1280, 1280], P('expert'), may hold values from -0.15625 to 0.15625
- w_output: bfloat16 [1280, 1280], P('expert'), may hold values from -2.5 to 2.5
- router: bfloat16 [1280, 16], P('expert'), may hold values from -0.078125 to 0.078125
- shared_gate: bfloat16 [1280, 896], P('expert'), may hold values from -0.15625 to 0.15625
- shared_up: bfloat16 [1280, 896], P('expert'), may hold values from -0.15625 to 0.15625
- shared_down: bfloat16 [896, 1280], P('expert'), may hold values from -0.1875 to 0.1875
- expert_gate: bfloat16 [16, 1280, 896], P('expert'), may hold values from -0.15625 to 0.15625
- expert_up: bfloat16 [16, 1280, 896], P('expert'), may hold values from -0.15625 to 0.15625
- expert_down: bfloat16 [16, 896, 1280], P('expert'), may hold values from -12 to 12
- expert_ids: int32 [32, 128, 6], P(('dp', 'expert')), may hold values from 0 to 15, all different within a row; in each aligned block of 128 rows (0 to 127, 128 to 255, ..., all dimensions but the last counted through in order) at most 96 rows name the same one
Outputs:
- layer_output: bfloat16 [4, 1024, 1280], P('dp', 'expert')
- input_grad: bfloat16 [4, 1024, 1280], P('dp', 'expert')
- attn_gain_grad: float32 [1280], P('expert')
- ffn_gain_grad: float32 [1280], P('expert')
- query_grad: float32 [1280, 1280], P('expert')
- key_grad: float32 [1280, 1280], P('expert')
- value_grad: float32 [1280, 1280], P('expert')
- output_grad: float32 [1280, 1280], P('expert')
- router_grad: float32 [1280, 16], P('expert')
- shared_gate_grad: float32 [1280, 896], P('expert')
- shared_up_grad: float32 [1280, 896], P('expert')
- shared_down_grad: float32 [896, 1280], P('expert')
- expert_gate_grad: float32 [16, 1280, 896], P('expert')
- expert_up_grad: float32 [16, 1280, 896], P('expert')
- expert_down_grad: float32 [16, 896, 1280], P('expert')
Inputs may be any that keep to these rules, and one draw needn't show every extreme that they name: `expert_ids`: in each block of 128 rows (one value of the first dimension) no expert is named more than 96 times, a bound that some block reaches; the 6 ids of a token differ.
All inputs are finite; a program needn't handle non-finite values.
Results may differ from a plain program's by a relative error of at most 0.02.
Values may be sent and summed in bfloat16 or wider, within the bound.
A program may use at most 320 MiB of HBM per device.

v0:
```python
import jax
import jax.numpy as jnp
from jax import lax
from jax.sharding import PartitionSpec as P

HEAD_DIM = 128


norm_eps = 1e-06
masked_score = -1e30


def rotary_tables(positions, head_size):
    half_size = head_size // 2
    inverse_freq = 10000.0 ** (-jnp.arange(half_size, dtype=jnp.float32) * 2.0 / head_size)
    angles = positions.astype(jnp.float32)[:, None] * inverse_freq[None, :]
    cosine = jnp.cos(angles)
    sine_part = jnp.sin(angles)
    return (
        jnp.concatenate([cosine, cosine], -1)[:, None, :],
        jnp.concatenate([sine_part, sine_part], -1)[:, None, :],
    )


def rotate(values, cosine, sine_part):
    half_size = values.shape[-1] // 2
    turned = jnp.concatenate([-values[..., half_size:], values[..., :half_size]], -1)
    return values * cosine + turned * sine_part


def rotate_back(grads, cosine, sine_part):
    half_size = grads.shape[-1] // 2
    scaled = grads * sine_part
    turned = jnp.concatenate([scaled[..., half_size:], -scaled[..., :half_size]], -1)
    return grads * cosine + turned


def norm_back(grad, values, inverse, gain):
    scaled = grad * gain
    inner = jnp.mean(scaled * values, -1, keepdims=True)
    return inverse * scaled - values * inverse**3 * inner


def swiglu_back(grad_hidden, gates, ups):
    sigma = jax.nn.sigmoid(gates)
    grad_gate = grad_hidden * ups * sigma * (1.0 + gates * (1.0 - sigma))
    grad_up = grad_hidden * (gates * sigma)
    return (grad_gate.astype(jnp.bfloat16), grad_up.astype(jnp.bfloat16))


def body(
    tokens,
    cotangent,
    attn_gain,
    ffn_gain,
    w_query,
    w_key,
    w_value,
    w_output,
    router,
    shared_gate,
    shared_up,
    shared_down,
    expert_gate,
    expert_up,
    expert_down,
    expert_ids,
):
    gathered = (
        lax.all_gather(attn_gain, "expert", axis=0, tiled=True),
        lax.all_gather(ffn_gain, "expert", axis=0, tiled=True),
        lax.all_gather(w_query, "expert", axis=0, tiled=True),
        lax.all_gather(w_key, "expert", axis=0, tiled=True),
        lax.all_gather(w_value, "expert", axis=0, tiled=True),
        lax.all_gather(w_output, "expert", axis=0, tiled=True),
        lax.all_gather(router, "expert", axis=0, tiled=True),
        lax.all_gather(shared_gate, "expert", axis=0, tiled=True),
        lax.all_gather(shared_up, "expert", axis=0, tiled=True),
        lax.all_gather(shared_down, "expert", axis=0, tiled=True),
    )
    (
        gain_one,
        gain_two,
        full_query,
        full_key,
        full_value,
        full_output,
        full_router,
        shared_gate_all,
        shared_up_all,
        shared_down_all,
    ) = gathered
    seq_count, pos_count, model_width = tokens.shape
    head_count = model_width // HEAD_DIM
    tok_rows = seq_count * pos_count
    route_top = expert_ids.shape[-1]
    expert_count = full_router.shape[1]
    local_experts = expert_gate.shape[0]
    group_count = lax.axis_size("expert")
    capacity = max(2, 2 * tok_rows * route_top // expert_count)
    score_scale = HEAD_DIM ** (-0.5)
    dev_index = lax.axis_index("expert")
    positions = dev_index * pos_count + jnp.arange(pos_count)
    cosine, sine_part = rotary_tables(positions, HEAD_DIM)
    shaped = (seq_count, pos_count, head_count, HEAD_DIM)
    inputs = tokens.astype(jnp.float32).reshape(tok_rows, model_width)
    gain_first = gain_one.astype(jnp.float32)
    gain_second = gain_two.astype(jnp.float32)
    inverse_one = lax.rsqrt(jnp.mean(inputs * inputs, -1, keepdims=True) + norm_eps)
    normed_one = (inputs * inverse_one * gain_first).astype(jnp.bfloat16)
    query_proj = jnp.dot(normed_one, full_query, preferred_element_type=jnp.float32)
    key_proj = jnp.dot(normed_one, full_key, preferred_element_type=jnp.float32)
    value_proj = jnp.dot(normed_one, full_value, preferred_element_type=jnp.float32)
    query_b = rotate(query_proj.reshape(shaped), cosine, sine_part).astype(jnp.bfloat16)
    key_b = rotate(key_proj.reshape(shaped), cosine, sine_part).astype(jnp.bfloat16)
    value_b = value_proj.reshape(shaped).astype(jnp.bfloat16)
    all_keys, all_values = (
        lax.all_gather(key_b, "expert", axis=1, tiled=True),
        lax.all_gather(value_b, "expert", axis=1, tiled=True),
    )
    length_all = all_keys.shape[1]
    allowed = jnp.arange(length_all)[None, :] <= positions[:, None]

    def scores_of(queries, keys_in, mask):
        raw = (
            jnp.einsum("sqhd,skhd->shqk", queries, keys_in, preferred_element_type=jnp.float32)
            * score_scale
        )
        return jnp.where(mask, raw, masked_score)

    scores = scores_of(query_b, all_keys, allowed)
    top_score = jnp.max(scores, -1, keepdims=True)
    raised = jnp.exp(scores - top_score)
    totals = jnp.sum(raised, -1, keepdims=True)
    probs = raised / totals
    log_total = top_score + jnp.log(totals)
    mixed = jnp.einsum(
        "shqk,skhd->sqhd",
        probs.astype(jnp.bfloat16),
        all_values,
        preferred_element_type=jnp.float32,
    )
    mixed_b = mixed.astype(jnp.bfloat16).reshape(tok_rows, model_width)
    attended = jnp.dot(mixed_b, full_output, preferred_element_type=jnp.float32)
    resid = inputs + attended
    inverse_two = lax.rsqrt(jnp.mean(resid * resid, -1, keepdims=True) + norm_eps)
    normed_two = (resid * inverse_two * gain_second).astype(jnp.bfloat16)
    logits = jnp.dot(normed_two, full_router, preferred_element_type=jnp.float32)
    probs_expert = jax.nn.softmax(logits, axis=-1)
    route_ids = expert_ids.reshape(tok_rows, route_top)
    onehot = (route_ids[:, :, None] == jnp.arange(expert_count)[None, None, :]).astype(jnp.float32)
    gate_vals = jnp.sum(onehot * probs_expert[:, None, :], -1)
    gate_shared = jnp.dot(normed_two, shared_gate_all, preferred_element_type=jnp.float32)
    up_shared = jnp.dot(normed_two, shared_up_all, preferred_element_type=jnp.float32)
    hidden_shared = (jax.nn.silu(gate_shared) * up_shared).astype(jnp.bfloat16)
    shared_out = jnp.dot(hidden_shared, shared_down_all, preferred_element_type=jnp.float32)
    flat_ids = route_ids.reshape(-1)
    flags = (flat_ids[:, None] == jnp.arange(expert_count)[None, :]).astype(jnp.int32)
    earlier = jnp.cumsum(flags, 0) - flags
    slots = jnp.sum(earlier * flags, 1)
    targets = flat_ids * capacity + slots
    buffer_shape = (group_count, local_experts, capacity, model_width)
    outgoing = (
        jnp.zeros((expert_count * capacity, model_width), jnp.bfloat16)
        .at[targets]
        .set(jnp.repeat(normed_two, route_top, 0))
    )
    arrived = lax.all_to_all(
        outgoing.reshape(buffer_shape), "expert", split_axis=0, concat_axis=0, tiled=True
    )
    gate_hidden = jnp.einsum(
        "sjcd,jdf->sjcf", arrived, expert_gate, preferred_element_type=jnp.float32
    )
    up_hidden = jnp.einsum("sjcd,jdf->sjcf", arrived, expert_up, preferred_element_type=jnp.float32)
    activated = (jax.nn.silu(gate_hidden) * up_hidden).astype(jnp.bfloat16)
    expert_out = jnp.einsum(
        "sjcf,jfd->sjcd", activated, expert_down, preferred_element_type=jnp.float32
    ).astype(jnp.bfloat16)
    returned = lax.all_to_all(expert_out, "expert", split_axis=0, concat_axis=0, tiled=True)
    picked = (
        returned.reshape(expert_count * capacity, model_width)[targets]
        .reshape(tok_rows, route_top, model_width)
        .astype(jnp.float32)
    )
    routed = jnp.sum(gate_vals[..., None] * picked, 1)
    layer_output = (resid + shared_out + routed).astype(jnp.bfloat16).reshape(tokens.shape)
    grad_out = cotangent.astype(jnp.float32).reshape(tok_rows, model_width)
    grad_out_b = grad_out.astype(jnp.bfloat16)
    shared_down_grad = jnp.einsum(
        "rf,rd->fd", hidden_shared, grad_out_b, preferred_element_type=jnp.float32
    )
    grad_hidden_shared = jnp.einsum(
        "rd,fd->rf", grad_out_b, shared_down_all, preferred_element_type=jnp.float32
    )
    grad_gate_shared, grad_up_shared = swiglu_back(grad_hidden_shared, gate_shared, up_shared)
    shared_gate_grad = jnp.einsum(
        "rd,rf->df", normed_two, grad_gate_shared, preferred_element_type=jnp.float32
    )
    shared_up_grad = jnp.einsum(
        "rd,rf->df", normed_two, grad_up_shared, preferred_element_type=jnp.float32
    )
    grad_gate_vals = jnp.sum(grad_out[:, None, :] * picked, -1)
    route_grads = (
        (gate_vals[..., None] * grad_out[:, None, :])
        .astype(jnp.bfloat16)
        .reshape(tok_rows * route_top, model_width)
    )
    grad_outgoing = (
        jnp.zeros((expert_count * capacity, model_width), jnp.bfloat16).at[targets].set(route_grads)
    )
    grad_arrived = lax.all_to_all(
        grad_outgoing.reshape(buffer_shape), "expert", split_axis=0, concat_axis=0, tiled=True
    )
    gate_again = jnp.einsum(
        "sjcd,jdf->sjcf", arrived, expert_gate, preferred_element_type=jnp.float32
    )
    up_again = jnp.einsum("sjcd,jdf->sjcf", arrived, expert_up, preferred_element_type=jnp.float32)
    activated_again = (jax.nn.silu(gate_again) * up_again).astype(jnp.bfloat16)
    expert_down_grad = jnp.einsum(
        "sjcf,sjcd->jfd", activated_again, grad_arrived, preferred_element_type=jnp.float32
    )
    grad_activated = jnp.einsum(
        "sjcd,jfd->sjcf", grad_arrived, expert_down, preferred_element_type=jnp.float32
    )
    grad_gate_routed, grad_up_routed = swiglu_back(grad_activated, gate_again, up_again)
    expert_gate_grad = jnp.einsum(
        "sjcd,sjcf->jdf", arrived, grad_gate_routed, preferred_element_type=jnp.float32
    )
    expert_up_grad = jnp.einsum(
        "sjcd,sjcf->jdf", arrived, grad_up_routed, preferred_element_type=jnp.float32
    )
    grad_rows = jnp.einsum(
        "sjcf,jdf->sjcd", grad_gate_routed, expert_gate, preferred_element_type=jnp.float32
    )
    grad_rows = grad_rows + jnp.einsum(
        "sjcf,jdf->sjcd", grad_up_routed, expert_up, preferred_element_type=jnp.float32
    )
    back_rows = lax.all_to_all(
        grad_rows.astype(jnp.bfloat16), "expert", split_axis=0, concat_axis=0, tiled=True
    )
    expert_gate_grad, expert_up_grad, expert_down_grad = lax.psum(
        (expert_gate_grad, expert_up_grad, expert_down_grad), "dp"
    )
    grad_probs_expert = jnp.sum(grad_gate_vals[..., None] * onehot, 1)
    grad_logits = probs_expert * (
        grad_probs_expert - jnp.sum(probs_expert * grad_probs_expert, -1, keepdims=True)
    )
    grad_logits = grad_logits.astype(jnp.bfloat16)
    router_grad = jnp.einsum(
        "rd,re->de", normed_two, grad_logits, preferred_element_type=jnp.float32
    )
    grad_normed_two = jnp.einsum(
        "rf,df->rd", grad_gate_shared, shared_gate_all, preferred_element_type=jnp.float32
    )
    grad_normed_two = grad_normed_two + jnp.einsum(
        "rf,df->rd", grad_up_shared, shared_up_all, preferred_element_type=jnp.float32
    )
    grad_normed_two = grad_normed_two + jnp.einsum(
        "re,de->rd", grad_logits, full_router, preferred_element_type=jnp.float32
    )
    routed_back = back_rows.reshape(expert_count * capacity, model_width)[targets].reshape(
        tok_rows, route_top, model_width
    )
    grad_normed_two = grad_normed_two + jnp.sum(routed_back.astype(jnp.float32), 1)
    ffn_gain_grad = jnp.sum(grad_normed_two * resid * inverse_two, 0)
    grad_resid = grad_out + norm_back(grad_normed_two, resid, inverse_two, gain_second)
    grad_attended = grad_resid.astype(jnp.bfloat16)
    output_grad = jnp.einsum(
        "rd,re->de", mixed_b, grad_attended, preferred_element_type=jnp.float32
    )
    grad_mixed = (
        jnp.einsum("re,de->rd", grad_attended, full_output, preferred_element_type=jnp.float32)
        .astype(jnp.bfloat16)
        .reshape(shaped)
    )
    scores = scores_of(query_b, all_keys, allowed)
    probs = jnp.exp(scores - log_total)
    grad_probs = jnp.einsum(
        "sqhd,skhd->shqk", grad_mixed, all_values, preferred_element_type=jnp.float32
    )
    delta = jnp.sum(probs * grad_probs, -1, keepdims=True)
    grad_scores = (probs * (grad_probs - delta)).astype(jnp.bfloat16)
    grad_query = score_scale * jnp.einsum(
        "shqk,skhd->sqhd", grad_scores, all_keys, preferred_element_type=jnp.float32
    )
    key_part = score_scale * jnp.einsum(
        "shqk,sqhd->skhd", grad_scores, query_b, preferred_element_type=jnp.float32
    )
    value_part = jnp.einsum(
        "shqk,sqhd->skhd",
        probs.astype(jnp.bfloat16),
        grad_mixed,
        preferred_element_type=jnp.float32,
    )
    grad_key, grad_value = (
        lax.psum_scatter(key_part, "expert", scatter_dimension=1, tiled=True),
        lax.psum_scatter(value_part, "expert", scatter_dimension=1, tiled=True),
    )
    grad_query_b = (
        rotate_back(grad_query, cosine, sine_part)
        .astype(jnp.bfloat16)
        .reshape(tok_rows, model_width)
    )
    grad_key_b = (
        rotate_back(grad_key, cosine, sine_part).astype(jnp.bfloat16).reshape(tok_rows, model_width)
    )
    grad_value_b = grad_value.astype(jnp.bfloat16).reshape(tok_rows, model_width)
    query_grad = jnp.einsum(
        "rd,re->de", normed_one, grad_query_b, preferred_element_type=jnp.float32
    )
    key_grad = jnp.einsum("rd,re->de", normed_one, grad_key_b, preferred_element_type=jnp.float32)
    value_grad = jnp.einsum(
        "rd,re->de", normed_one, grad_value_b, preferred_element_type=jnp.float32
    )
    grad_normed_one = jnp.einsum(
        "re,de->rd", grad_query_b, full_query, preferred_element_type=jnp.float32
    )
    grad_normed_one = grad_normed_one + jnp.einsum(
        "re,de->rd", grad_key_b, full_key, preferred_element_type=jnp.float32
    )
    grad_normed_one = grad_normed_one + jnp.einsum(
        "re,de->rd", grad_value_b, full_value, preferred_element_type=jnp.float32
    )
    attn_gain_grad = jnp.sum(grad_normed_one * inputs * inverse_one, 0)
    grad_inputs = grad_resid + norm_back(grad_normed_one, inputs, inverse_one, gain_first)
    input_grad = grad_inputs.astype(jnp.bfloat16).reshape(tokens.shape)
    dense_parts = (
        lax.psum_scatter(attn_gain_grad, "expert", scatter_dimension=0, tiled=True),
        lax.psum_scatter(ffn_gain_grad, "expert", scatter_dimension=0, tiled=True),
        lax.psum_scatter(query_grad, "expert", scatter_dimension=0, tiled=True),
        lax.psum_scatter(key_grad, "expert", scatter_dimension=0, tiled=True),
        lax.psum_scatter(value_grad, "expert", scatter_dimension=0, tiled=True),
        lax.psum_scatter(output_grad, "expert", scatter_dimension=0, tiled=True),
        lax.psum_scatter(router_grad, "expert", scatter_dimension=0, tiled=True),
        lax.psum_scatter(shared_gate_grad, "expert", scatter_dimension=0, tiled=True),
        lax.psum_scatter(shared_up_grad, "expert", scatter_dimension=0, tiled=True),
        lax.psum_scatter(shared_down_grad, "expert", scatter_dimension=0, tiled=True),
    )
    dense_parts = lax.psum(
        (
            dense_parts[0],
            dense_parts[1],
            dense_parts[2],
            dense_parts[3],
            dense_parts[4],
            dense_parts[5],
            dense_parts[6],
            dense_parts[7],
            dense_parts[8],
            dense_parts[9],
        ),
        "dp",
    )
    return (
        layer_output,
        input_grad,
        dense_parts[0],
        dense_parts[1],
        dense_parts[2],
        dense_parts[3],
        dense_parts[4],
        dense_parts[5],
        dense_parts[6],
        dense_parts[7],
        dense_parts[8],
        dense_parts[9],
        expert_gate_grad,
        expert_up_grad,
        expert_down_grad,
    )


def solution(mesh):
    placed = (
        P("dp", "expert", None),
        P("dp", "expert", None),
        P("expert"),
        P("expert"),
        P("expert", None),
        P("expert", None),
        P("expert", None),
        P("expert", None),
        P("expert", None),
        P("expert", None),
        P("expert", None),
        P("expert", None),
        P("expert", None, None),
        P("expert", None, None),
        P("expert", None, None),
        P(("dp", "expert"), None, None),
    )
    return jax.shard_map(
        body,
        mesh=mesh,
        in_specs=placed,
        out_specs=(
            P("dp", "expert", None),
            P("dp", "expert", None),
            P("expert"),
            P("expert"),
            P("expert", None),
            P("expert", None),
            P("expert", None),
            P("expert", None),
            P("expert", None),
            P("expert", None),
            P("expert", None),
            P("expert", None),
            P("expert", None, None),
            P("expert", None, None),
            P("expert", None, None),
        ),
        check_vma=False,
    )
```

profile of v0, /device:TPU:13, one launch (start us, length us, event | category | flops | bytes accessed | tf_op | source)
XLA Modules:
  0.0 1984.4 jit_solution(7488926355817630756)
XLA Ops:
  13.1 11.5 all-reduce.7
  27.4 22.5 %all-gather.16.cloned.1.call-done = bf16[1280,1280]{1,0:T(8,128)(2,1)} async-done(((bf16[160,1280]{1,0:T(8,128)(2,1)}), bf16[1280,1280]{1,0:T(8,128)(2,1)}) %all-gather.16.cloned.1.call-update) | async-done | bytes 3276816 | tf_op jit(solution)/shard_map/all_gather | solution.py:73
  49.9 3.5 fusion.103
  54.9 34.9 %all-gather.12.cloned.1.call-done = bf16[1280,1280]{1,0:T(8,128)(2,1)} async-done(((bf16[160,1280]{1,0:T(8,128)(2,1)}), bf16[1280,1280]{1,0:T(8,128)(2,1)}) %all-gather.12.cloned.1.call-update) | async-done | bytes 3276816 | tf_op jit(solution)/shard_map/all_gather | solution.py:74
  89.8 5.6 copy.173
  95.5 3.9 convolution_convert_fusion.1
  103.1 26.6 %all-gather.14.cloned.1.call-done = bf16[1280,1280]{1,0:T(8,128)(2,1)} async-done(((bf16[160,1280]{1,0:T(8,128)(2,1)}), bf16[1280,1280]{1,0:T(8,128)(2,1)}) %all-gather.14.cloned.1.call-update) | async-done | bytes 3276816 | tf_op jit(solution)/shard_map/all_gather | solution.py:72
  129.7 3.3 fusion.105
  133.3 31.6 %all-gather.18.cloned.1.call-done = bf16[1,1024,10,128]{3,1,2,0:T(8,128)(2,1)} async-done(((bf16[1,128,10,128]{3,1,2,0:T(8,128)(2,1)}), bf16[1,1024,10,128]{3,1,2,0:T(8,128)(2,1)}) %all-gather.18.cloned.1.call-update) | async-done | bytes 2621456 | tf_op jit(solution)/shard_map/all_gather | solution.py:118
  170.7 29.2 %all-gather.28.cloned.1.call-done = bf16[1024,10,128]{2,0,1:T(8,128)(2,1)} async-done(((bf16[128,10,128]{2,0,1:T(8,128)(2,1)}), bf16[1024,10,128]{2,0,1:T(8,128)(2,1)}) %all-gather.28.cloned.1.call-update) | async-done | bytes 2621456 | tf_op jit(solution)/shard_map/all_gather | solution.py:119
  199.8 4.8 fusion.62
  204.6 34.7 %all-gather.20.cloned.1.call-done = bf16[1280,1280]{1,0:T(8,128)(2,1)} async-done(((bf16[160,1280]{1,0:T(8,128)(2,1)}), bf16[1280,1280]{1,0:T(8,128)(2,1)}) %all-gather.20.cloned.1.call-update) | async-done | bytes 3276816 | tf_op jit(solution)/shard_map/all_gather | solution.py:75
  247.7 8.3 scatter_custom_fusion
  256.1 6.0 all-to-all-start
  262.1 93.5 %all-gather.1 = bf16[8,160,16]{1,2,0:T(8,128)(2,1)S(1)} all-gather(bf16[1,160,16]{1,2,0:T(8,128)(2,1)S(1)} %bitcast.292), channel_id=1, replica_groups=mesh['dp'=4,'expert'=8] {'expert'}, dimensions={0}, use_global_device_ids=true | all-gather | bytes 46080 | tf_op jit(solution)/shard_map/all_gather | solution.py:76
  359.3 5.0 mul.445
  365.4 13.0 scatter_custom_fusion.1
  378.3 5.5 all-to-all-start.2
  384.5 10.2 fusion.11
  394.7 10.3 fusion.15
  405.1 82.0 %all-to-all-done.2 = bf16[8,2,96,1280]{3,2,1,0:T(8,128)(2,1)} async-done(((bf16[8,2,96,1280]{3,2,1,0:T(8,128)(2,1)}), bf16[8,2,96,1280]{3,2,1,0:T(8,128)(2,1)}, u32[]{:S(2)}, u32[]{:S(2)}) %all-to-all-start.2) | async-done | bytes 3932192 | tf_op jit(solution)/shard_map/all_to_all | solution.py:211
  487.1 11.9 fusion.3
  498.9 7.8 fusion.28
  508.9 8.1 all-to-all-start.1
  517.7 7.4 fusion.13
  525.1 7.6 fusion.25
  534.9 85.3 %all-to-all-done.1 = bf16[8,2,96,1280]{3,2,1,0:T(8,128)(2,1)} async-done(((bf16[8,2,96,1280]{3,2,1,0:T(8,128)(2,1)}), bf16[8,2,96,1280]{3,2,1,0:T(8,128)(2,1)}, u32[]{:S(2)}, u32[]{:S(2)}) %all-to-all-start.1) | async-done | bytes 3932192 | tf_op jit(solution)/shard_map/all_to_all | solution.py:179
  620.3 8.1 all-to-all-start.3
  634.8 45.5 %all-gather.26.cloned.1.call-done = bf16[896,1280]{1,0:T(8,128)(2,1)} async-done(((bf16[112,1280]{1,0:T(8,128)(2,1)}), bf16[896,1280]{1,0:T(8,128)(2,1)}) %all-gather.26.cloned.1.call-update) | async-done | bytes 2293776 | tf_op jit(solution)/shard_map/all_gather | solution.py:79
  680.3 3.3 multiply_convert_fusion.4
  686.0 7.2 gather_fusion
  696.0 5.0 multiply_reduce_fusion.1
  701.8 29.8 %all-to-all-done.3 = bf16[8,2,96,1280]{3,2,1,0:T(8,128)(2,1)} async-done(((bf16[8,2,96,1280]{3,2,1,0:T(8,128)(2,1)}), bf16[8,2,96,1280]{3,2,1,0:T(8,128)(2,1)}, u32[]{:S(2)}, u32[]{:S(2)}) %all-to-all-start.3) | async-done | bytes 3932192 | tf_op jit(solution)/shard_map/all_to_all | solution.py:238
  731.6 7.2 gather_fusion.1
  741.6 4.1 reduce_sum.157
  749.3 5.7 fusion.47
  755.3 4.3 multiply_reduce_fusion
  759.6 3.6 multiply_convert_fusion
  766.4 3.9 fusion.129
  774.2 3.9 fusion.89
  778.1 5.0 fusion.100
  789.2 3.9 fusion.96
  793.2 22.0 %reduce-scatter.15.cloned.1.call-done = f32[1,128,10,128]{1,3,2,0:T(8,128)} async-done(((f32[1,1024,10,128]{1,3,2,0:T(8,128)}), f32[1,128,10,128]{1,3,2,0:T(8,128)}) %reduce-scatter.15.cloned.1.call-update) | async-done | bytes 655376 | tf_op jit(solution)/shard_map/reduce_scatter | solution.py:297
  816.3 3.8 fusion.98
  820.2 56.2 %reduce-scatter.13.cloned.1.call-done = f32[1,128,10,128]{3,1,2,0:T(8,128)} async-done(((f32[1,1024,10,128]{3,1,2,0:T(8,128)}), f32[1,128,10,128]{3,1,2,0:T(8,128)}) %reduce-scatter.13.cloned.1.call-update) | async-done | bytes 655376 | tf_op jit(solution)/shard_map/reduce_scatter | solution.py:296
  878.3 3.9 fusion.94
  882.7 11.4 convolution_bitcast_fusion.1
  894.1 8.6 convolution_bitcast_fusion.2
  904.1 10.5 convolution_bitcast_fusion
  914.6 16.1 reduce-scatter.27.cloned.1.call-done
  930.7 54.5 %reduce-scatter.25.cloned.1.call-done = f32[160,896]{1,0:T(8,128)} async-done(((f32[1280,896]{1,0:T(8,128)}), f32[160,896]{1,0:T(8,128)}) %reduce-scatter.25.cloned.1.call-update) | async-done | bytes 573456 | tf_op jit(solution)/shard_map/reduce_scatter | solution.py:335
  985.1 54.2 %reduce-scatter.29.cloned.1.call-done = f32[112,1280]{1,0:T(8,128)} async-done(((f32[896,1280]{1,0:T(8,128)}), f32[112,1280]{1,0:T(8,128)}) %reduce-scatter.29.cloned.1.call-update) | async-done | bytes 573456 | tf_op jit(solution)/shard_map/reduce_scatter | solution.py:337
  1039.4 72.9 %reduce-scatter.23.cloned.1.call-done = f32[160,1280]{1,0:T(8,128)} async-done(((f32[1280,1280]{1,0:T(8,128)}), f32[160,1280]{1,0:T(8,128)}) %reduce-scatter.23.cloned.1.call-update) | async-done | bytes 819216 | tf_op jit(solution)/shard_map/reduce_scatter | solution.py:333
  1112.3 72.9 %reduce-scatter.17.cloned.1.call-done = f32[160,1280]{1,0:T(8,128)} async-done(((f32[1280,1280]{1,0:T(8,128)}), f32[160,1280]{1,0:T(8,128)}) %reduce-scatter.17.cloned.1.call-update) | async-done | bytes 819216 | tf_op jit(solution)/shard_map/reduce_scatter | solution.py:330
  1185.2 72.9 %reduce-scatter.21.cloned.1.call-done = f32[160,1280]{1,0:T(8,128)} async-done(((f32[1280,1280]{1,0:T(8,128)}), f32[160,1280]{1,0:T(8,128)}) %reduce-scatter.21.cloned.1.call-update) | async-done | bytes 819216 | tf_op jit(solution)/shard_map/reduce_scatter | solution.py:332
  1258.2 72.9 %reduce-scatter.19.cloned.1.call-done = f32[160,1280]{1,0:T(8,128)} async-done(((f32[1280,1280]{1,0:T(8,128)}), f32[160,1280]{1,0:T(8,128)}) %reduce-scatter.19.cloned.1.call-update) | async-done | bytes 819216 | tf_op jit(solution)/shard_map/reduce_scatter | solution.py:331
  1336.8 21.7 %reduce-scatter.31.cloned.1.call-done = f32[160,16]{1,0:T(8,128)} async-done(((f32[1280,16]{1,0:T(8,128)}), f32[160,16]{1,0:T(8,128)}) %reduce-scatter.31.cloned.1.call-update) | async-done | bytes 10256
  1359.5 3.3 convolution_add_fusion.1
  1364.2 27.6 %all-reduce.4 = (f32[1280]{0:T(1024)S(1)}, f32[1280]{0:T(1024)S(1)}) all-reduce(f32[1280]{0:T(1024)S(1)} %get-tuple-element.19, f32[1280]{0:T(1024)S(1)} %copy-done.43), channel_id=5, replica_groups=mesh['dp'=4,'expert'=8] {'expert'}, use_global_device_ids=true, to_apply=%region_23.24.clone | all-reduce | flops 2560 | bytes 20480
  1392.0 13.8 all-reduce.5
  1406.8 541.7 %all-reduce.10.cloned.1.call-done = (f32[160,1280]{1,0:T(8,128)}, f32[160,1280]{1,0:T(8,128)}, f32[160,1280]{1,0:T(8,128)}, f32[160,1280]{1,0:T(8,128)}, f32[160...) async-done(((f32[160,1280]{1,0:T(8,128)}, ...) | async-done | bytes 32522256 | tf_op jit(solution)/shard_map/psum | solution.py:339
  1958.3 9.0 copy.273
  1967.3 4.7 copy.274
  1973.7 3.7 copy.275
  (261 shorter events, 95.3 us)
Async XLA Ops:
  7.2 42.8 %all-gather.16.cloned.1.call-start = ((), (), s32[]{:S(2)}) async-start(), calls=%async_computation.16 | async-start | bytes 3686400 | tf_op jit(solution)/shard_map/all_gather | solution.py:73
  7.9 81.9 %all-gather.12.cloned.1.call-start = ((), (), s32[]{:S(2)}) async-start(), calls=%async_computation.14 | async-start | bytes 3686400 | tf_op jit(solution)/shard_map/all_gather | solution.py:74
  8.7 121.1 %all-gather.14.cloned.1.call-start = ((), (), s32[]{:S(2)}) async-start(), calls=%async_computation.15 | async-start | bytes 3686400 | tf_op jit(solution)/shard_map/all_gather | solution.py:72
  9.4 155.5 %all-gather.18.cloned.1.call-start = ((), (), s32[]{:S(2)}) async-start(), calls=%async_computation.17 | async-start | bytes 2949120 | tf_op jit(solution)/shard_map/all_gather | solution.py:118
  24.6 105.1 %copy-start.21 = (f32[1280]{0:T(1024)}, f32[1280]{0:T(1024)S(1)}, u32[]{:S(2)}) copy-start(f32[1280]{0:T(1024)S(1)} %convert_element_type.161) | copy-start | bytes 15364
  25.7 74.6 %copy-start.25 = (f32[128,128]{1,0:T(8,128)}, f32[128,128]{1,0:T(8,128)S(1)}, u32[]{:S(2)}) copy-start(f32[128,128]{1,0:T(8,128)S(1)} %get-tuple-element.55) | copy-start | bytes 196612
  25.7 74.7 %copy-start.23 = (f32[128,128]{1,0:T(8,128)}, f32[128,128]{1,0:T(8,128)S(1)}, u32[]{:S(2)}) copy-start(f32[128,128]{1,0:T(8,128)S(1)} %get-tuple-element.76) | copy-start | bytes 196612
  27.4 102.3 %copy-start.38 = (f32[128]{0:T(128)}, f32[128]{0:T(128)S(1)}, u32[]{:S(2)}) copy-start(f32[128]{0:T(128)S(1)} %get-tuple-element.61) | copy-start | bytes 1540
  54.9 40.6 %copy-start.1 = (bf16[1,128,1280]{2,1,0:T(8,128)(2,1)S(1)}, bf16[1,128,1280]{2,1,0:T(8,128)(2,1)}, u32[]{:S(2)}) copy-start(bf16[1,128,1280]{2,1,0:T(8,128)(2,1)} %param.16) | copy-start | bytes 983044
  54.9 144.9 %all-gather.28.cloned.1.call-start = ((), (), s32[]{:S(2)}) async-start(), calls=%async_computation.31 | async-start | bytes 2949120 | tf_op jit(solution)/shard_map/all_gather | solution.py:119
  95.5 4.5 copy-start.44
  99.4 140.0 %all-gather.20.cloned.1.call-start = ((), (), s32[]{:S(2)}) async-start(), calls=%async_computation.18 | async-start | bytes 3686400 | tf_op jit(solution)/shard_map/all_gather | solution.py:75
  100.6 142.0 %copy-start.36 = (f32[1280]{0:T(1024)}, f32[1280]{0:T(1024)S(1)}, u32[]{:S(2)}) copy-start(f32[1280]{0:T(1024)S(1)} %convert_element_type.174) | copy-start | bytes 15364
  133.2 34.3 %copy-start.19 = (bf16[128,10,128]{0,2,1:T(8,128)(2,1)}, bf16[128,10,128]{0,2,1:T(8,128)(2,1)S(1)}, u32[]{:S(2)}) copy-start(bf16[128,10,128]{0,2,1:T(8,128)(2,1)S(1)} %fusion.83) | copy-start | bytes 983044
  204.6 38.0 %copy-start.18 = (bf16[10,128,128]{2,1,0:T(8,128)(2,1)}, bf16[10,128,128]{2,1,0:T(8,128)(2,1)S(1)}, u32[]{:S(2)}) copy-start(bf16[10,128,128]{2,1,0:T(8,128)(2,1)S(1)} %fusion.62) | copy-start | bytes 983044
  242.0 504.8 %copy-start.2 = (f32[128,1280]{1,0:T(8,128)}, f32[128,1280]{1,0:T(8,128)S(1)}, u32[]{:S(2)}) copy-start(f32[128,1280]{1,0:T(8,128)S(1)} %get-tuple-element.67) | copy-start | bytes 1966084
  256.1 6.0 copy-start.47
  256.1 99.6 %copy-start.13 = (bf16[1,128,1280]{2,1,0:T(8,128)(2,1)S(1)}, bf16[1,128,1280]{2,1,0:T(8,128)(2,1)}, u32[]{:S(2)}) copy-start(bf16[1,128,1280]{2,1,0:T(8,128)(2,1)} %param.17) | copy-start | bytes 983044
  256.1 122.3 %all-to-all-start = ((bf16[8,2,96,1280]{3,2,1,0:T(8,128)(2,1)}), bf16[8,2,96,1280]{3,2,1,0:T(8,128)(2,1)}, u32[]{:S(2)}, u32[]{:S(2)}) async-start(bf16[8,2,96,1280]{3,2,1,0:T(8,128)(2,1)} %bitcast.271), calls=%async_computation | async-start | bytes 7864320 | tf_op jit(solution)/shard_map/all_to_all | solution.py:168
  262.1 103.0 %copy-start.41 = (s32[1,128,6]{1,2,0:T(8,128)}, s32[1,128,6]{1,2,0:T(8,128)S(1)}, u32[]{:S(2)}) copy-start(s32[1,128,6]{1,2,0:T(8,128)S(1)} %copy.251) | copy-start | bytes 9220
  365.2 13.1 copy-start.30
  378.3 108.7 %all-to-all-start.2 = ((bf16[8,2,96,1280]{3,2,1,0:T(8,128)(2,1)}), bf16[8,2,96,1280]{3,2,1,0:T(8,128)(2,1)}, u32[]{:S(2)}, u32[]{:S(2)}) async-start(bf16[8,2,96,1280]{3,2,1,0:T(8,128)(2,1)} %bitcast.270), calls=%async_computation.2 | async-start | bytes 7864320 | tf_op jit(solution)/shard_map/all_to_all | solution.py:211
  383.8 246.7 %all-gather.24.cloned.1.call-start = ((), (), s32[]{:S(2)}) async-start(), calls=%async_computation.20 | async-start | bytes 2580480 | tf_op jit(solution)/shard_map/all_gather | solution.py:78
  498.9 7.8 copy-start.55
  508.9 111.3 %all-to-all-start.1 = ((bf16[8,2,96,1280]{3,2,1,0:T(8,128)(2,1)}), bf16[8,2,96,1280]{3,2,1,0:T(8,128)(2,1)}, u32[]{:S(2)}, u32[]{:S(2)}) async-start(bf16[8,2,96,1280]{3,2,1,0:T(8,128)(2,1)} %copy.194), calls=%async_computation.1 | async-start | bytes 7864320 | tf_op jit(solution)/shard_map/all_to_all | solution.py:179
  517.0 115.7 %all-gather.22.cloned.1.call-start = ((), (), s32[]{:S(2)}) async-start(), calls=%async_computation.19 | async-start | bytes 2580480 | tf_op jit(solution)/shard_map/all_gather | solution.py:77
  620.3 111.3 %all-to-all-start.3 = ((bf16[8,2,96,1280]{3,2,1,0:T(8,128)(2,1)}), bf16[8,2,96,1280]{3,2,1,0:T(8,128)(2,1)}, u32[]{:S(2)}, u32[]{:S(2)}) async-start(bf16[8,2,96,1280]{3,2,1,0:T(8,128)(2,1)} %copy.198), calls=%async_computation.3 | async-start | bytes 7864320 | tf_op jit(solution)/shard_map/all_to_all | solution.py:238
  628.3 52.0 %all-gather.26.cloned.1.call-start = ((), (), s32[]{:S(2)}) async-start(), calls=%async_computation.21 | async-start | bytes 2580480 | tf_op jit(solution)/shard_map/all_gather | solution.py:79
  629.1 186.1 %reduce-scatter.15.cloned.1.call-start = ((), (), s32[]{:S(2)}) async-start(), calls=%async_computation.23 | async-start | bytes 5898240 | tf_op jit(solution)/shard_map/reduce_scatter | solution.py:297
  680.3 4.1 copy-start.10
  696.0 5.1 copy-start.42
  696.0 5.1 copy-start.46
  696.0 5.1 copy-start.49
  741.6 4.2 copy-start.17
  741.6 4.2 copy-start.37
  741.6 4.2 copy-start.40
  741.6 4.2 copy-start.51
  741.6 5.2 copy-start.14
  741.6 5.2 copy-start.52
  755.0 121.4 %reduce-scatter.13.cloned.1.call-start = ((), (), s32[]{:S(2)}) async-start(), calls=%async_computation.22 | async-start | bytes 5898240 | tf_op jit(solution)/shard_map/reduce_scatter | solution.py:296
  766.4 164.3 %reduce-scatter.27.cloned.1.call-start = ((), (), s32[]{:S(2)}) async-start(), calls=%async_computation.29 | async-start | bytes 5160960 | tf_op jit(solution)/shard_map/reduce_scatter | solution.py:336
  770.4 214.8 %reduce-scatter.25.cloned.1.call-start = ((), (), s32[]{:S(2)}) async-start(), calls=%async_computation.28 | async-start | bytes 5160960 | tf_op jit(solution)/shard_map/reduce_scatter | solution.py:335
  773.3 266.1 %reduce-scatter.29.cloned.1.call-start = ((), (), s32[]{:S(2)}) async-start(), calls=%async_computation.30 | async-start | bytes 5160960 | tf_op jit(solution)/shard_map/reduce_scatter | solution.py:337
  778.1 334.2 %reduce-scatter.23.cloned.1.call-start = ((), (), s32[]{:S(2)}) async-start(), calls=%async_computation.27 | async-start | bytes 7372800 | tf_op jit(solution)/shard_map/reduce_scatter | solution.py:333
  783.1 402.1 %reduce-scatter.17.cloned.1.call-start = ((), (), s32[]{:S(2)}) async-start(), calls=%async_computation.24 | async-start | bytes 7372800 | tf_op jit(solution)/shard_map/reduce_scatter | solution.py:330
  793.2 465.0 %reduce-scatter.21.cloned.1.call-start = ((), (), s32[]{:S(2)}) async-start(), calls=%async_computation.26 | async-start | bytes 7372800 | tf_op jit(solution)/shard_map/reduce_scatter | solution.py:332
  820.1 56.3 %copy-start.26 = (f32[128,128]{1,0:T(8,128)S(1)}, f32[128,128]{1,0:T(8,128)}, u32[]{:S(2)}) copy-start(f32[128,128]{1,0:T(8,128)} %copy-done.25) | copy-start | bytes 196612
  820.1 57.7 %copy-start.24 = (f32[128,128]{1,0:T(8,128)S(1)}, f32[128,128]{1,0:T(8,128)}, u32[]{:S(2)}) copy-start(f32[128,128]{1,0:T(8,128)} %copy-done.23) | copy-start | bytes 196612
  820.1 511.0 %reduce-scatter.19.cloned.1.call-start = ((), (), s32[]{:S(2)}) async-start(), calls=%async_computation.25 | async-start | bytes 7372800 | tf_op jit(solution)/shard_map/reduce_scatter | solution.py:331
  882.2 476.3 %reduce-scatter.31.cloned.1.call-start = ((), (), s32[]{:S(2)}) async-start(), calls=%async_computation.32 | async-start | bytes 737280
  882.7 11.4 copy-start.54
  903.9 1044.6 %all-reduce.10.cloned.1.call-start = ((), (), s32[]{:S(2)}) async-start(), calls=%async_computation.33 | async-start | bytes 65044480 | tf_op jit(solution)/shard_map/psum | solution.py:339
  1331.9 3.7 copy-start.6
  1359.5 4.7 copy-start.43
  1359.5 46.2 %copy-start.8 = (f32[128,1280]{1,0:T(8,128)S(1)}, f32[128,1280]{1,0:T(8,128)}, u32[]{:S(2)}) copy-start(f32[128,1280]{1,0:T(8,128)} %copy-done.7) | copy-start | bytes 1966084
  1359.5 46.2 %copy-start.53 = (f32[128]{0:T(128)S(1)}, f32[128]{0:T(128)}, u32[]{:S(2)}) copy-start(f32[128]{0:T(128)} %get-tuple-element.60) | copy-start | bytes 1540
  1948.5 6.5 copy-start.29
  1948.5 7.4 copy-start.33
  1948.5 8.2 copy-start.32
  1950.7 6.8 copy-start.31
  1958.3 9.0 copy-start.9
  1958.3 13.7 slice-start
  1958.3 15.2 slice-start.1
  1967.3 6.5 slice-start.2
  (19 other events, 36.3 us)
Sparse Core Ops, SparseCore 0:
  9.7 40.2 all-gather.15
  51.6 38.2 all-gather.11
  91.5 38.2 all-gather.13
  131.8 33.0 all-gather.17
  166.9 32.8 all-gather.27
  201.3 37.9 all-gather.19
  386.3 49.4 all-gather.23
  519.5 49.4 all-gather.21
  630.8 49.4 all-gather.25
  755.1 60.0 reduce-scatter.14
  818.1 58.2 reduce-scatter.12
  878.6 52.0 reduce-scatter.26
  933.1 51.9 reduce-scatter.24
  987.3 52.0 reduce-scatter.28
  1041.7 70.5 reduce-scatter.22
  1114.6 70.6 reduce-scatter.16
  1187.5 70.6 reduce-scatter.20
  1260.5 70.6 reduce-scatter.18
  1334.1 24.4 reduce-scatter.30
  1365.2 583.1 all-reduce.9
where the time goes:
time: 1990 us; the launch traced here: 1980 us
  waiting for transfers between devices  1480 us (74%)
  matrix products  172 us (9%)
  blocking collectives  146 us (7%)
  local copies, waits for them, and re-layouts  95.5 us (5%)
  other arithmetic  39.3 us (2%)
  starting transfers between devices  30.2 us (2%)
    psum x1, waiting for transfers between devices, body(): lax.psum((dense_parts[0], dense_parts[1], dense_parts[2], dense_parts[3],...  542 us
    all_gather x1, blocking collectives, body(): lax.all_gather(router, 'expert', axis=0, tiled=True)  93.5 us
    all_to_all x1, waiting for transfers between devices, body(): lax.all_to_all(expert_out, 'expert', split_axis=0, concat_axis=0, tiled=T...  85.3 us
    all_to_all x1, waiting for transfers between devices, body(): lax.all_to_all(grad_outgoing.reshape(buffer_shape), 'expert', split_axis=...  82 us
    reduce_scatter x1, waiting for transfers between devices, body(): lax.psum_scatter(query_grad, 'expert', scatter_dimension=0, tiled=True)  72.9 us
    reduce_scatter x1, waiting for transfers between devices, body(): lax.psum_scatter(key_grad, 'expert', scatter_dimension=0, tiled=True)  72.9 us
    reduce_scatter x1, waiting for transfers between devices, body(): lax.psum_scatter(value_grad, 'expert', scatter_dimension=0, tiled=True)  72.9 us
    reduce_scatter x1, waiting for transfers between devices, body(): lax.psum_scatter(output_grad, 'expert', scatter_dimension=0, tiled=True)  72.9 us
  transfers between devices with their start and end apart: 24, of which 21 were waited for; matrix products, arithmetic and copies ran while one was open for 12% of the time, Pallas kernels for 0%

commit v1 on v0

v1 whole, which is shorter than its diff:
```python
import functools

import jax
import jax.numpy as jnp
from jax import lax
from jax.experimental import pallas as pl
from jax.experimental.pallas import tpu as pltpu
from jax.sharding import PartitionSpec as P

HEAD_DIM = 128
LANES = 128
EPS = 1e-06
MASKED = -1e30
VMEM_LIMIT = 60 * 2**20
BF = jnp.bfloat16
F32 = jnp.float32


def dot(a, b):
    return jnp.dot(a, b, preferred_element_type=F32)


def dot_nt(a, b):
    return lax.dot_general(a, b, (((1,), (1,)), ((), ())), preferred_element_type=F32)


def dot_tn(a, b):
    return lax.dot_general(a, b, (((0,), (0,)), ((), ())), preferred_element_type=F32)


def silu(v):
    return v / (1.0 + jnp.exp(-v))


def swiglu_back(d_hidden, gates, ups):
    sigma = 1.0 / (1.0 + jnp.exp(-gates))
    d_gate = d_hidden * ups * sigma * (1.0 + gates * (1.0 - sigma))
    d_up = d_hidden * (gates * sigma)
    return d_gate.astype(BF), d_up.astype(BF)


def rotary_tables(length):
    half = HEAD_DIM // 2
    inverse_freq = 10000.0 ** (-jnp.arange(half, dtype=F32) * 2.0 / HEAD_DIM)
    angles = jnp.arange(length).astype(F32)[:, None] * inverse_freq[None, :]
    cosine, sine = jnp.cos(angles), jnp.sin(angles)
    return jnp.concatenate([cosine, cosine], -1), jnp.concatenate([-sine, sine], -1)


def vmem_call(kernel, outs, *args, remote_id=None, **kwargs):
    spec = pl.BlockSpec(memory_space=pltpu.VMEM)
    params = {} if remote_id is None else {"collective_id": remote_id, "has_side_effects": True}
    return pl.pallas_call(
        kernel,
        out_shape=outs,
        in_specs=[spec] * len(args),
        out_specs=[spec] * len(outs),
        compiler_params=pltpu.CompilerParams(vmem_limit_bytes=VMEM_LIMIT, **params),
        **kwargs,
    )(*args)


def row_block(length):
    return 256 if length % 256 == 0 else length


def remote(src, dst, send, recv, **device):
    return pltpu.make_async_remote_copy(
        src_ref=src, dst_ref=dst, send_sem=send, recv_sem=recv, device_id=device, device_id_type=pl.DeviceIdType.MESH
    )


def meet(peers):
    barrier = pltpu.get_barrier_semaphore()
    for peer in peers:
        pl.semaphore_signal(barrier, inc=1, device_id=peer, device_id_type=pl.DeviceIdType.MESH)
    pl.semaphore_wait(barrier, len(peers))


def meet_near(chips, z, me, peers=()):
    barrier = pltpu.get_barrier_semaphore()
    near = [(True, {"expert": me + 1 - 2 * lax.rem(me, 2)}), (z > 0, {"expert": me - 2}), (z < chips - 1, {"expert": me + 2})]
    near += [(True, {"dp": t}) for t in peers]

    def signal(t):
        pl.semaphore_signal(barrier, inc=1, device_id=t, device_id_type=pl.DeviceIdType.MESH)

    for ok, t in near:
        guarded(ok, functools.partial(signal, t))
    ends = jnp.where(z > 0, 1, 0) + jnp.where(z < chips - 1, 1, 0)
    pl.semaphore_wait(barrier, 1 + len(peers) + ends)


def both(*conditions):
    held = [c for c in conditions if c is not True]
    if not held:
        return True
    out = held[0]
    for c in held[1:]:
        out = jnp.logical_and(out, c)
    return out


def guarded(condition, action):
    if condition is True:
        action()
    else:
        pl.when(condition)(action)


class LineGather:
    def __init__(self, ranks, own, block, send, recv, base=0, valid=lambda i: True, twins=True):
        self.me = lax.axis_index("expert")
        self.chips = ranks // 2
        self.z = self.me // 2
        self.twin = self.me + 1 - 2 * lax.rem(self.me, 2)
        self.own, self.block, self.send, self.recv, self.base, self.valid = own, block, send, recv, base, valid
        self.twins = twins

    @staticmethod
    def semaphores(ranks):
        return 4 * (ranks // 2 - 1) + 1

    def copy(self, src, i, k, to):
        return remote(src, self.block(i), self.send.at[self.base + k], self.recv.at[self.base + k], expert=to)

    def sources(self, s):
        hops = self.chips - 1
        return (
            (self.me - 2 * s, self.z - s >= 0, self.z < hops, self.me + 2, 0, 2 * hops, -2 * s),
            (self.me + 2 * s, self.z + s <= hops, self.z > 0, self.me - 2, hops, 3 * hops, 2 * s),
        )

    def start(self):
        hops = self.chips - 1
        mine = self.valid(self.me)
        if hops:
            guarded(both(self.z < hops, mine), lambda: self.copy(self.own, self.me, 0, self.me + 2).start())
            guarded(both(self.z > 0, mine), lambda: self.copy(self.own, self.me, hops, self.me - 2).start())
        if self.twins:
            guarded(mine, lambda: self.copy(self.own, self.me, 2 * hops, self.twin).start())

    def step(self, s):
        for i, there, more, to, k, pair, _ in self.sources(s):
            known = both(there, self.valid(i))
            src = self.block(i)
            guarded(known, lambda: self.copy(src, i, k + s - 1, self.twin).wait_recv())
            if s < self.chips - 1:
                guarded(both(known, more), lambda: self.copy(src, i, k + s, to).start())
            if self.twins:
                guarded(known, lambda: self.copy(src, i, pair + s, self.twin).start())

    def finish(self):
        hops = self.chips - 1
        mine = self.valid(self.me)
        theirs = self.valid(self.twin)
        if self.twins:
            guarded(mine, lambda: self.copy(self.own, self.me, 2 * hops, self.twin).wait_send())
            guarded(theirs, lambda: self.copy(self.own, self.twin, 2 * hops, self.twin).wait_recv())
        if hops:
            guarded(both(self.z < hops, mine), lambda: self.copy(self.own, self.me, 0, self.twin).wait_send())
            guarded(both(self.z > 0, mine), lambda: self.copy(self.own, self.me, hops, self.twin).wait_send())
        for s in range(1, self.chips):
            for i, there, more, to, k, pair, shift in self.sources(s):
                known = both(there, self.valid(i))
                src = self.block(i)
                if s < hops:
                    guarded(both(known, more), lambda: self.copy(src, i, k + s, self.twin).wait_send())
                if not self.twins:
                    continue
                guarded(known, lambda: self.copy(src, i, pair + s, self.twin).wait_send())
                j = self.twin + shift
                got = both(there, self.valid(j))
                guarded(got, lambda: self.copy(self.block(j), j, pair + s, self.twin).wait_recv())


class Across:
    SEMAPHORES = 12

    def __init__(self, source, dst, send, recv):
        self.me, self.g = lax.axis_index("expert"), lax.axis_index("dp")
        self.twin = self.me + 1 - 2 * lax.rem(self.me, 2)
        self.by_x = self.g + 1 - 2 * lax.rem(self.g, 2)
        self.by_y = lax.rem(self.g + 2, 4)
        self.source, self.dst, self.send, self.recv = source, dst, send, recv
        self.half = dst.shape[1]
        self.part = self.half // 2

    def peers(self):
        return [{"dp": self.by_x}, {"dp": self.by_y}, {"expert": self.twin}]

    def piece(self, slot, j):
        return self.dst.at[slot, pl.ds(j * self.part, self.part)]

    def mine(self, j):
        first = lax.rem(self.me, 2) * self.half + j * self.part
        return self.source(pl.ds(pl.multiple_of(first, self.part), self.part))

    def copy(self, k, src, dst, **to):
        return remote(src, dst, self.send.at[k], self.recv.at[k], **to)

    def direct(self, k):
        slot, j, to = ((0, 0, self.by_x), (1, 1, self.by_y), (0, 1, self.by_x), (1, 0, self.by_y))[k]
        return self.copy(k, self.mine(j), self.piece(slot, j), dp=to)

    def relayed(self, j):
        if j == 0:
            return self.copy(4, self.piece(0, 0), self.piece(2, 0), dp=self.by_y)
        return self.copy(5, self.piece(1, 1), self.piece(2, 1), dp=self.by_x)

    def shared(self, slot, j):
        return self.copy(6 + 2 * slot + j, self.piece(slot, j), self.piece(slot + 3, j), expert=self.twin)

    def start(self):
        for k in range(4):
            self.direct(k).start()

    def relay(self):
        self.direct(0).wait_recv()
        self.relayed(0).start()
        self.direct(1).wait_recv()
        self.relayed(1).start()
        self.shared(0, 0).start()
        self.shared(1, 1).start()

    def hand_over(self):
        self.direct(2).wait_recv()
        self.shared(0, 1).start()
        self.direct(3).wait_recv()
        self.shared(1, 0).start()

    def finish(self):
        for j in range(2):
            self.relayed(j).wait_recv()
            self.shared(2, j).start()
        for k in range(4):
            self.direct(k).wait_send()
        for j in range(2):
            self.relayed(j).wait_send()
            for slot in range(3):
                self.shared(slot, j).wait()


class SameExperts:
    SEMAPHORES = 6

    def __init__(self, source, dst, send, recv):
        self.me, self.g = lax.axis_index("expert"), lax.axis_index("dp")
        self.near = [self.g + 1 - 2 * lax.rem(self.g, 2), lax.rem(self.g + 2, 4)]
        self.near.append(self.near[1] + 1 - 2 * lax.rem(self.near[1], 2))
        self.source, self.dst, self.send, self.recv = source, dst, send, recv
        self.half = dst.shape[1]

    def peers(self):
        return [{"dp": self.near[2]}]

    def copy(self, k, h):
        slot = k + 3 * lax.rem(lax.rem(self.me, 2) + h, 2)
        i = 2 * k + h
        src = self.source.at[pl.ds(h * self.half, self.half)]
        return remote(src, self.dst.at[slot], self.send.at[i], self.recv.at[i], dp=self.near[k])

    def start(self):
        for k in range(3):
            for h in range(2):
                self.copy(k, h).start()

    def relay(self):
        pass

    hand_over = relay

    def finish(self):
        for k in range(3):
            for h in range(2):
                self.copy(k, h).wait()


def aligned(i, size):
    return pl.ds(pl.multiple_of(i * size, size), size)


def front_kernel(
    ranks, groups, heads, slots, x_ref, wq_ref, wk_ref, wv_ref, pack_ref,
    gx_ref, w_ref, stage_ref, land_ref,
    x_send, x_recv, w_send, w_recv, d_send, d_recv,
):
    me, g = lax.axis_index("expert"), lax.axis_index("dp")
    rows = wq_ref.shape[0]
    peers = [lax.rem(g + d, groups) for d in range(1, groups)]
    others = [lax.rem(me + d, ranks) for d in range(1, ranks)]
    meet([{"expert": t} for t in others] + [{"dp": t} for t in peers])

    tokens = LineGather(ranks, x_ref, lambda i: gx_ref.at[i], x_send, x_recv)
    tokens.start()

    def stage_heads(w):
        for u in range(heads):
            stage_ref[u] = w[:, u * LANES : (u + 1) * LANES]

    for which, w in enumerate((wq_ref, wk_ref, wv_ref)):
        pl.when(g == which)(functools.partial(stage_heads, w))

    def stage_pack():
        for s in range(slots):
            stage_ref[pl.ds(s * ranks, ranks)] = pack_ref[:, :, s * LANES : (s + 1) * LANES]

    pl.when(g == groups - 1)(stage_pack)

    def known(s, t, group=None):
        return jnp.logical_or((g if group is None else group) == groups - 1, s * ranks + t < heads)

    def weight_copy(s, d, unit, i, to):
        return remote(
            stage_ref.at[unit], land_ref.at[g, s, i], w_send.at[s, d], w_recv.at[s, d], expert=to
        )

    for d in range(1, ranks):
        t = others[d - 1]
        for s in range(slots):
            guarded(known(s, t), lambda: weight_copy(s, d, s * ranks + t, me, t).start())
    for s in range(slots):
        def keep(s=s):
            land_ref[g, s, me] = stage_ref[s * ranks + me]

        pl.when(known(s, me))(keep)
        for which in range(groups - 1):
            def clear(s=s, which=which):
                land_ref[which, s] = jnp.zeros(land_ref.shape[2:], BF)

            pl.when(s * ranks + me >= heads)(clear)

    gx_ref[me] = x_ref[...]

    def share(s, part, d, to):
        return remote(part, part, d_send.at[s, d], d_recv.at[s, d], dp=to)

    def pass_on(i):
        for s in range(slots):
            part = land_ref.at[g, s, i]
            for d in range(1, groups):
                pl.when(known(s, me))(lambda: share(s, part, d, peers[d - 1]).start())

    pass_on(me)
    steps = ranks // 2 - 1
    taken = 1
    for step in range(1, steps + 1):
        tokens.step(step)
        until = ranks if step == steps else min(ranks, taken + 2)
        for d in range(taken, until):
            i = lax.rem(me + ranks - d, ranks)
            for s in range(slots):
                pl.when(known(s, me))(lambda: weight_copy(s, d, 0, i, others[0]).wait_recv())
            pass_on(i)
        taken = until
    tokens.finish()
    for d in range(1, ranks):
        t = others[d - 1]
        for s in range(slots):
            pl.when(known(s, t))(lambda: weight_copy(s, d, 0, me, t).wait_send())
    for d in range(1, groups):
        there = lax.rem(g + groups - d, groups)
        for s in range(slots):
            pl.when(known(s, me))(lambda: share(s, land_ref.at[g, s], d, peers[d - 1]).wait_send())
            pl.when(known(s, me, there))(lambda: share(s, land_ref.at[there, s], d, peers[d - 1]).wait_recv())
    for which in range(groups):
        for s in range(slots):
            for r in range(ranks):
                w_ref[which, r * rows : (r + 1) * rows, s * LANES : (s + 1) * LANES] = land_ref[which, s, r]


def front(ranks, groups, heads, slots, x, w_query, w_key, w_value, pack):
    own, width = x.shape
    rows = w_query.shape[0]
    line = LineGather.semaphores(ranks)
    dma = pltpu.SemaphoreType.DMA
    spec = pl.BlockSpec(memory_space=pltpu.VMEM)
    shape = jax.ShapeDtypeStruct
    return pl.pallas_call(
        functools.partial(front_kernel, ranks, groups, heads, slots),
        out_shape=[
            shape((ranks, own, width), BF),
            shape((groups, width, slots * LANES), BF),
        ],
        in_specs=[spec] * 5,
        out_specs=[spec] * 2,
        scratch_shapes=[
            pltpu.VMEM((slots * ranks, rows, LANES), BF),
            pltpu.VMEM((groups, slots, ranks, rows, LANES), BF),
            dma((line,)), dma((line,)),
            dma((slots, ranks)), dma((slots, ranks)),
            dma((slots, groups)), dma((slots, groups)),
        ],
        compiler_params=pltpu.CompilerParams(
            collective_id=0, has_side_effects=True, vmem_limit_bytes=VMEM_LIMIT
        ),
        name="front",
    )(x, w_query, w_key, w_value, pack)


def project_kernel(
    ranks, heads, slots, x_ref, mixed_ref, half_ref, gain_ref, c_ref,
    resid_ref, n_ref, all_ref, wo_ref, c_all_ref, other_ref, send, recv, t_send, t_recv, a_send, a_recv,
):
    me = lax.axis_index("expert")
    chips = ranks // 2
    z = me // 2
    share = c_all_ref.shape[-1]
    across = Across(lambda r: c_ref.at[r, pl.ds(0, share)], c_all_ref, a_send, a_recv)
    meet_near(chips, z, me, [across.by_x, across.by_y])
    twin = me + 1 - 2 * lax.rem(me, 2)
    halves = remote(half_ref, other_ref, t_send, t_recv, expert=twin)
    halves.start()
    across.start()
    line = LineGather.semaphores(ranks)
    parts = []
    for s in range(slots):
        def head(i, s=s):
            return aligned(jnp.clip(s * ranks + i, 0, heads - 1), LANES)

        cols = slice(s * LANES, (s + 1) * LANES)
        ok = (lambda i: True) if (s + 1) * ranks <= heads else (lambda i, s=s: s * ranks + i < heads)
        gather = LineGather(
            ranks, mixed_ref.at[:, cols], lambda i, head=head: all_ref.at[:, head(i)], send, recv, s * line, ok
        )
        gather.start()
        parts.append(gather)

        def keep(cols=cols, head=head):
            all_ref[:, head(me)] = mixed_ref[:, cols]

        guarded(ok(me), keep)
    for step in range(1, chips):
        for gather in parts:
            gather.step(step)
    for gather in parts:
        gather.finish()
    across.relay()
    halves.wait()
    groups, per, _, part, _ = half_ref.shape

    def lay_out(even, odd):
        for which in range(groups):
            for k in range(per):
                u = which * per + k
                if u < wo_ref.shape[1] // LANES:
                    cols = slice(u * LANES, (u + 1) * LANES)
                    for c in range(chips):
                        wo_ref[2 * c * part : (2 * c + 1) * part, cols] = even[which, k, c]
                        wo_ref[(2 * c + 1) * part : (2 * c + 2) * part, cols] = odd[which, k, c]

    pl.when(me == 2 * z)(lambda: lay_out(half_ref, other_ref))
    pl.when(me != 2 * z)(lambda: lay_out(other_ref, half_ref))
    blocks, own, width = x_ref.shape
    gain = gain_ref[...]
    tile = 2 if own <= 128 and blocks % 2 == 0 else 1

    def rows_of(b):
        rows = aligned(b, tile * own)
        x = x_ref[pl.ds(b * tile, tile)].reshape(tile * own, width).astype(F32)
        resid = x + dot(all_ref[rows, :], wo_ref[...])
        inverse = lax.rsqrt(jnp.mean(resid * resid, -1, keepdims=True) + EPS)
        n_ref[rows, :] = (resid * inverse * gain).astype(BF)
        for t in range(tile):
            def keep(t=t):
                resid_ref[...] = resid[t * own : (t + 1) * own]

            pl.when(b * tile + t == me)(keep)

    lax.fori_loop(0, blocks // tile, lambda b, c: (rows_of(b), c)[1], 0)
    across.hand_over()
    across.finish()


def project(ranks, heads, slots, x, mixed, half, gain, cot):
    blocks, own, width = x.shape
    total = blocks * own
    line = LineGather.semaphores(ranks)
    dma = pltpu.SemaphoreType.DMA
    spec = pl.BlockSpec(memory_space=pltpu.VMEM)
    anywhere = pl.BlockSpec(memory_space=pl.ANY)
    shape = jax.ShapeDtypeStruct
    return pl.pallas_call(
        functools.partial(project_kernel, ranks, heads, slots),
        out_shape=[
            shape((own, width), F32),
            shape((total, width), BF),
            shape((total, width), BF),
            shape((width, width), BF),
            shape((6, total // 2, width // 2), BF),
        ],
        in_specs=[spec] * 4 + [anywhere],
        out_specs=[spec] * 4 + [anywhere],
        scratch_shapes=[
            pltpu.VMEM(half.shape, BF), dma((slots * line,)), dma((slots * line,)), dma(()), dma(()),
            dma((Across.SEMAPHORES,)), dma((Across.SEMAPHORES,)),
        ],
        compiler_params=pltpu.CompilerParams(
            collective_id=2, has_side_effects=True, vmem_limit_bytes=VMEM_LIMIT
        ),
        name="project",
    )(x, mixed, half, gain, cot)


def attend_kernel(
    ranks, groups, seqs, slots, x_ref, gain_ref, wq_ref, wk_ref, wv_ref, cos_ref, sin_ref, wo_ref,
    inv_ref, q_ref, k_ref, v_ref, mixed_ref, lse_ref, half_ref,
    stage_ref, o_send, o_recv, p_send, p_recv,
):
    total, width = x_ref.shape
    length = total // seqs
    block = row_block(length)
    scale = HEAD_DIM ** (-0.5)

    me, g = lax.axis_index("expert"), lax.axis_index("dp")
    chips, per = half_ref.shape[2], half_ref.shape[1]
    z = me // 2
    peers = [lax.rem(g + d, groups) for d in range(1, groups)]
    meet_near(chips, z, me, peers)
    for which in range(groups):

        def stage(which=which):
            for k in range(per):
                u = which * per + k
                if u < width // LANES:
                    stage_ref[k] = wo_ref[:, u * LANES : (u + 1) * LANES]

        pl.when(g == which)(stage)
    out_rows = LineGather(
        ranks, stage_ref, lambda i: half_ref.at[g, :, i // 2], o_send, o_recv, twins=False
    )
    out_rows.start()
    half_ref[g, :, z] = stage_ref[...]

    def out_share(d, group, to):
        part = half_ref.at[group]
        return remote(part, part, p_send.at[d], p_recv.at[d], dp=to)

    pending = list(range(1, chips))

    def progress():
        if pending:
            out_rows.step(pending.pop(0))
            if not pending:
                out_rows.finish()
                for d in range(1, groups):
                    out_share(d, g, peers[d - 1]).start()

    for s in range(seqs):
        for i in range(length // block):
            rows = pl.ds(s * length + i * block, block)
            x = x_ref[rows, :].astype(F32)
            inv = lax.rsqrt(jnp.mean(x * x, -1, keepdims=True) + EPS)
            normed = (x * inv * gain_ref[...].astype(F32)).astype(BF)
            inv_ref[rows, :] = inv
            cosine = cos_ref[pl.ds(i * block, block), :]
            sine = sin_ref[pl.ds(i * block, block), :]
            queries, keyed, valued = dot(normed, wq_ref[...]), dot(normed, wk_ref[...]), dot(normed, wv_ref[...])
            for h in range(slots):
                cols = slice(h * HEAD_DIM, (h + 1) * HEAD_DIM)
                q, k = queries[:, cols], keyed[:, cols]
                q_ref[rows, cols] = (q * cosine + pltpu.roll(q, HEAD_DIM // 2, 1) * sine).astype(BF)
                k_ref[rows, cols] = (k * cosine + pltpu.roll(k, HEAD_DIM // 2, 1) * sine).astype(BF)
            v_ref[rows, :] = valued.astype(BF)
    progress()
    for s in range(seqs):
        for i in range(length // block):
            if i:
                progress()
            rows = pl.ds(s * length + i * block, block)
            keys = pl.ds(s * length, (i + 1) * block)
            shape = (block, (i + 1) * block)
            seen = (
                lax.broadcasted_iota(jnp.int32, shape, 1)
                <= lax.broadcasted_iota(jnp.int32, shape, 0) + i * block
            )
            for h in range(slots):
                cols = slice(h * HEAD_DIM, (h + 1) * HEAD_DIM)
                scores = dot_nt(q_ref[rows, cols], k_ref[keys, cols]) * scale
                scores = jnp.where(seen, scores, MASKED)
                top = jnp.max(scores, -1, keepdims=True)
                raised = jnp.exp(scores - top)
                totals = jnp.sum(raised, -1, keepdims=True)
                probs = (raised / totals).astype(BF)
                mixed_ref[rows, cols] = dot(probs, v_ref[keys, cols]).astype(BF)
                lse_ref[rows, h : h + 1] = top + jnp.log(totals)
    while pending:
        progress()
    for d in range(1, groups):
        out_share(d, g, peers[d - 1]).wait_send()
        out_share(d, lax.rem(g + groups - d, groups), peers[d - 1]).wait_recv()


def attend(ranks, groups, seqs, slots, x, gain, w_q, w_k, w_v, cosine, sine, w_output):
    total, width = x.shape
    span = slots * HEAD_DIM
    rows = w_output.shape[0]
    per = -(-(width // LANES) // groups)
    line = LineGather.semaphores(ranks)
    dma = pltpu.SemaphoreType.DMA
    shape = jax.ShapeDtypeStruct
    return vmem_call(
        functools.partial(attend_kernel, ranks, groups, seqs, slots),
        [
            shape((total, 1), F32),
            shape((total, span), BF),
            shape((total, span), BF),
            shape((total, span), BF),
            shape((total, span), BF),
            shape((total, slots), F32),
            shape((groups, per, ranks // 2, rows, LANES), BF),
        ],
        x, gain, w_q, w_k, w_v, cosine, sine, w_output,
        scratch_shapes=[
            pltpu.VMEM((per, rows, LANES), BF),
            dma((line,)), dma((line,)),
            dma((groups,)), dma((groups,)),
        ],
        remote_id=1,
        name="attend",
    )


def attend_back_kernel(
    seqs, slots, da_ref, x_ref, inv_ref, g_ref, wq_ref, wk_ref, wv_ref, wo_ref, cos_ref, sin_ref,
    q_ref, k_ref, v_ref, lse_ref,
    dn_ref, dwq_ref, dwk_ref, dwv_ref, gain_ref, dmix_ref, dqkv_ref, dk_ref, dv_ref,
):
    total, width = da_ref.shape
    length = total // seqs
    block = row_block(length)
    count = length // block
    scale = HEAD_DIM ** (-0.5)
    span = slots * HEAD_DIM
    for s in range(seqs):
        for i in range(count):
            rows = pl.ds(s * length + i * block, block)
            dmix_ref[rows, :] = dot_nt(da_ref[rows, :], wo_ref[...]).astype(BF)
        for h in range(slots):
            cols = slice(h * HEAD_DIM, (h + 1) * HEAD_DIM)
            dk_ref[...] = jnp.zeros_like(dk_ref)
            dv_ref[...] = jnp.zeros_like(dv_ref)
            for i in range(count):
                rows = pl.ds(s * length + i * block, block)
                reach = (i + 1) * block
                keys = pl.ds(s * length, reach)
                shape = (block, reach)
                seen = (
                    lax.broadcasted_iota(jnp.int32, shape, 1)
                    <= lax.broadcasted_iota(jnp.int32, shape, 0) + i * block
                )
                q = q_ref[rows, cols]
                k = k_ref[keys, cols]
                dmix = dmix_ref[rows, cols]
                scores = jnp.where(seen, dot_nt(q, k) * scale, MASKED)
                probs = jnp.exp(scores - lse_ref[rows, h : h + 1])
                dp = dot_nt(dmix, v_ref[keys, cols])
                delta = jnp.sum(probs * dp, -1, keepdims=True)
                ds = (probs * (dp - delta)).astype(BF)
                dq = dot(ds, k) * scale
                cosine = cos_ref[pl.ds(i * block, block), :]
                sine = sin_ref[pl.ds(i * block, block), :]
                dqkv_ref[rows, h * HEAD_DIM : (h + 1) * HEAD_DIM] = (
                    dq * cosine - pltpu.roll(dq, HEAD_DIM // 2, 1) * sine
                ).astype(BF)
                dk_ref[pl.ds(0, reach), :] += dot_tn(ds, q)
                dv_ref[pl.ds(0, reach), :] += dot_tn(probs.astype(BF), dmix)
            for i in range(count):
                rows = pl.ds(s * length + i * block, block)
                here = pl.ds(i * block, block)
                dk = dk_ref[here, :] * scale
                dk = dk * cos_ref[here, :] - pltpu.roll(dk, HEAD_DIM // 2, 1) * sin_ref[here, :]
                dqkv_ref[rows, span + h * HEAD_DIM : span + (h + 1) * HEAD_DIM] = dk.astype(BF)
                dqkv_ref[rows, 2 * span + h * HEAD_DIM : 2 * span + (h + 1) * HEAD_DIM] = dv_ref[here, :].astype(BF)
    gain = jnp.zeros((1, width), F32)
    for i in range(total // block):
        rows = pl.ds(i * block, block)
        d_normed = dot_nt(dqkv_ref[rows, :span], wq_ref[...])
        d_normed += dot_nt(dqkv_ref[rows, span : 2 * span], wk_ref[...])
        d_normed += dot_nt(dqkv_ref[rows, 2 * span :], wv_ref[...])
        dn_ref[rows, :] = d_normed.astype(BF)
        gain += jnp.sum(d_normed * x_ref[rows, :].astype(F32) * inv_ref[rows, :], 0, keepdims=True)
    gain_ref[...] = gain
    step = LANES * 2
    for i in range(width // step):
        cols = slice(i * step, (i + 1) * step)
        normed = (x_ref[:, cols].astype(F32) * inv_ref[...] * g_ref[:, cols].astype(F32)).astype(BF)
        grads = dot_tn(normed, dqkv_ref[...]).astype(BF)
        dwq_ref[cols, :] = grads[:, :span]
        dwk_ref[cols, :] = grads[:, span : 2 * span]
        dwv_ref[cols, :] = grads[:, 2 * span :]


def attend_back(seqs, slots, d_att, x, inverse, gain, w_slices, w_out, cosine, sine, q, k, v, lse):
    total, width = d_att.shape
    span = slots * HEAD_DIM
    shape = jax.ShapeDtypeStruct
    return vmem_call(
        functools.partial(attend_back_kernel, seqs, slots),
        [shape((total, width), BF)] + [shape((width, span), BF)] * 3 + [shape((1, width), F32)],
        d_att, x, inverse, gain, *w_slices, w_out, cosine, sine, q, k, v, lse,
        scratch_shapes=[
            pltpu.VMEM((total, span), BF),
            pltpu.VMEM((total, 3 * span), BF),
            pltpu.VMEM((total // seqs, HEAD_DIM), F32),
            pltpu.VMEM((total // seqs, HEAD_DIM), F32),
        ],
        name="attend_back",
    )


def experts_kernel(
    experts, steps, n_ref, c_ref, prob_ref, weight_ref, eye_ref, wg_ref, wu_ref, wd_ref, sg_ref, su_ref, sd_ref,
    router_ref, n_group, c_group, w_group,
    out_ref, dx_ref, dlog_ref, dsg_ref, dsu_ref, dsd_ref, n_all, c_all, w_all, send, recv,
):
    step = pl.program_id(0)
    part = c_all.shape[-1]
    moves = [
        Across(lambda r: n_group.at[r], n_all, send.at[0], recv.at[0]),
        SameExperts(w_group, w_all, send.at[1], recv.at[1]),
        Across(lambda r: c_group.at[r, pl.ds(part, part)], c_all, send.at[2], recv.at[2]),
    ]

    @pl.when(step == 0)
    def _():
        meet(moves[0].peers() + moves[1].peers())
        for move in moves:
            move.start()

    @pl.when(step == steps // 3)
    def _():
        for move in moves:
            move.relay()

    @pl.when(step == 2 * steps // 3)
    def _():
        for move in moves:
            move.hand_over()

    n = n_ref[...]
    c_b = c_ref[...]
    c = c_b.astype(F32)
    gate = dot(n, sg_ref[...])
    up = dot(n, su_ref[...])
    hidden = (silu(gate) * up).astype(BF)
    out = dot(hidden, sd_ref[...])
    d_gate, d_up = swiglu_back(dot_nt(c_b, sd_ref[...]), gate, up)
    dx = dot_nt(d_gate, sg_ref[...]) + dot_nt(d_up, su_ref[...])

    @pl.when(step == 0)
    def _():
        dsg_ref[...] = jnp.zeros_like(dsg_ref)
        dsu_ref[...] = jnp.zeros_like(dsu_ref)
        dsd_ref[...] = jnp.zeros_like(dsd_ref)

    dsg_ref[...] += dot_tn(n, d_gate)
    dsu_ref[...] += dot_tn(n, d_up)
    dsd_ref[...] += dot_tn(hidden, c_b)
    probs = prob_ref[...]
    d_log = jnp.zeros_like(probs)
    inner = jnp.zeros((n.shape[0], 1), F32)
    for j in range(experts):
        weight = weight_ref[:, j : j + 1]
        gate = dot(n, wg_ref[j])
        up = dot(n, wu_ref[j])
        hidden = (silu(gate) * up).astype(BF)
        y = dot(hidden, wd_ref[j]).astype(BF).astype(F32)
        out += weight * y
        d_weight = weight * jnp.sum(c * y, -1, keepdims=True)
        d_log += eye_ref[j : j + 1, :] * d_weight
        inner += d_weight
        d_gate, d_up = swiglu_back(dot_nt((weight * c).astype(BF), wd_ref[j]), gate, up)
        dx += dot_nt(d_gate, wg_ref[j]) + dot_nt(d_up, wu_ref[j])
    d_log = (d_log - probs * inner).astype(BF)
    dlog_ref[...] = d_log
    dx += dot_nt(d_log, router_ref[...])
    out_ref[...] = out.astype(BF)
    dx_ref[...] = dx.astype(BF)

    @pl.when(step == steps - 1)
    def _():
        for move in moves:
            move.finish()


def experts(normed, cot, probs, weight, packed, eye, w_gate, w_up, w_down, s_gate, s_up, s_down, router):
    total, width = normed.shape
    count, _, hidden = w_gate.shape
    tile = 256 if total % 256 == 0 else total
    steps = total // tile
    anywhere = pl.BlockSpec(memory_space=pl.ANY)
    dma = pltpu.SemaphoreType.DMA
    names = probs.shape[1]
    share = s_gate.shape[1]

    def rows(cols):
        return pl.BlockSpec((tile, cols), lambda i: (i, 0))

    def whole(a):
        zeros = (0,) * a.ndim
        return pl.BlockSpec(a.shape, lambda i: zeros, pipeline_mode=pl.Buffered(1))

    shape = jax.ShapeDtypeStruct
    fixed = (eye, w_gate, w_up, w_down, s_gate, s_up, s_down, router)
    flops = total * width * hidden * count * 12
    return pl.pallas_call(
        functools.partial(experts_kernel, count, steps),
        grid=(steps,),
        in_specs=[rows(width), rows(width), rows(names), rows(count)] + [whole(a) for a in fixed] + [anywhere] * 3,
        out_specs=[
            rows(width),
            rows(width),
            rows(names),
            pl.BlockSpec((width, share), lambda i: (0, 0)),
            pl.BlockSpec((width, share), lambda i: (0, 0)),
            pl.BlockSpec((share, width), lambda i: (0, 0)),
            anywhere, anywhere, anywhere,
        ],
        out_shape=[
            shape((total, width), BF),
            shape((total, width), BF),
            shape((total, names), BF),
            shape((width, share), F32),
            shape((width, share), F32),
            shape((share, width), F32),
            shape((6, total // 2, width), BF),
            shape((6, total // 2, width // 2), BF),
            shape((6, total // 2, LANES), BF),
        ],
        scratch_shapes=[dma((3, Across.SEMAPHORES)), dma((3, Across.SEMAPHORES))],
        compiler_params=pltpu.CompilerParams(
            vmem_limit_bytes=VMEM_LIMIT, collective_id=3, has_side_effects=True
        ),
        cost_estimate=pl.CostEstimate(flops=flops, bytes_accessed=30 * 2**20, transcendentals=0),
        name="experts",
    )(normed, cot, probs, weight, *fixed, normed, cot, packed)


def routed_tile(j, count, n, c1, c2, packed, w_gate, w_up, w_down, acc_gate, acc_up, acc_down):
    part = c1.shape[-1]
    weight = packed[:, j : j + 1].astype(F32) + packed[:, count + j : count + j + 1].astype(F32)
    d_y = jnp.concatenate(
        [(weight * c1.astype(F32)).astype(BF), (weight * c2.astype(F32)).astype(BF)], -1
    )
    gate, up = dot(n, w_gate), dot(n, w_up)
    d_gate, d_up = swiglu_back(dot_nt(d_y, w_down), gate, up)
    hidden = (silu(gate) * up).astype(BF)
    acc_gate[...] += dot_tn(n, d_gate)
    acc_up[...] += dot_tn(n, d_up)
    acc_down[...] += dot_tn(hidden, d_y)


def weights_kernel(
    j, count, first, size, own_steps, n_own, c_own, packed_own, n_ref, c1_ref, c2_ref, packed_ref,
    wg_ref, wu_ref, wd_ref, *refs,
):
    dg_ref, du_ref, dd_ref, wg, wu, wd, acc_gate, acc_up, acc_down, load, store = refs[-11:]
    step = pl.program_id(0)
    cols = pl.ds(first, size)

    @pl.when(step == 0)
    def _():
        copies = [
            pltpu.make_async_copy(wg_ref.at[j, :, cols], wg, load.at[0]),
            pltpu.make_async_copy(wu_ref.at[j, :, cols], wu, load.at[1]),
            pltpu.make_async_copy(wd_ref.at[j, cols], wd, load.at[2]),
        ]
        for copy in copies:
            copy.start()
        for acc in (acc_gate, acc_up, acc_down):
            acc[...] = jnp.zeros_like(acc)
        for copy in copies:
            copy.wait()

    ours = step < own_steps
    part = c1_ref.shape[-1]
    routed_tile(
        j, count,
        jnp.where(ours, n_own[...], n_ref[0]),
        jnp.where(ours, c_own[:, :part], c1_ref[0]),
        jnp.where(ours, c_own[:, part : 2 * part], c2_ref[0]),
        jnp.where(ours, packed_own[...], packed_ref[0]),
        wg[...], wu[...], wd[...], acc_gate, acc_up, acc_down,
    )

    @pl.when(step == pl.num_programs(0) - 1)
    def _():
        copies = [
            pltpu.make_async_copy(acc_gate, dg_ref.at[j, :, cols], store.at[0]),
            pltpu.make_async_copy(acc_up, du_ref.at[j, :, cols], store.at[1]),
            pltpu.make_async_copy(acc_down, dd_ref.at[j, cols], store.at[2]),
        ]
        for copy in copies:
            copy.start()
        for copy in copies:
            copy.wait()


def expert_weights(j, first, size, tokens, weights, grads=None):
    own, others = tokens
    slots, half, width = others[0].shape
    count = weights[0].shape[0]
    tile = min(512, half)
    per = half // tile
    own_steps = 2 * per

    def own_rows(a):
        return pl.BlockSpec((tile, a.shape[-1]), lambda i: (jnp.minimum(i, own_steps - 1), 0))

    def rows(a):
        def place(i):
            k = jnp.maximum(i - own_steps, 0)
            return k // per, k % per, 0

        return pl.BlockSpec((1, tile, a.shape[-1]), place)

    anywhere = pl.BlockSpec(memory_space=pl.ANY)
    dma = pltpu.SemaphoreType.DMA
    before = [] if grads is None else list(grads)
    return pl.pallas_call(
        functools.partial(weights_kernel, j, count, first, size, own_steps),
        grid=(own_steps + slots * per,),
        in_specs=[own_rows(a) for a in own] + [rows(a) for a in others]
        + [anywhere] * (3 + len(before)),
        out_specs=[anywhere] * 3,
        out_shape=[jax.ShapeDtypeStruct(w.shape, F32) for w in weights],
        scratch_shapes=[
            pltpu.VMEM((width, size), BF), pltpu.VMEM((width, size), BF), pltpu.VMEM((size, width), BF),
            pltpu.VMEM((width, size), F32), pltpu.VMEM((width, size), F32), pltpu.VMEM((size, width), F32),
            dma((3,)), dma((3,)),
        ],
        input_output_aliases={} if grads is None else {10: 0, 11: 1, 12: 2},
        compiler_params=pltpu.CompilerParams(vmem_limit_bytes=VMEM_LIMIT),
        cost_estimate=pl.CostEstimate(
            flops=slots * half * width * size * 12, bytes_accessed=40 * 2**20, transcendentals=0
        ),
        name="expert_weights",
    )(*own, *others, *weights, *before)


def norm_back(grad, values, inverse, gain):
    scaled = grad * gain
    inner = jnp.mean(scaled * values, -1, keepdims=True)
    return inverse * scaled - values * inverse**3 * inner


def body(
    tokens, cotangent, attn_gain, ffn_gain, w_query, w_key, w_value, w_output, router,
    shared_gate, shared_up, shared_down, expert_gate, expert_up, expert_down, expert_ids,
):
    ranks = lax.axis_size("expert")
    me = lax.axis_index("expert")
    seqs, own_pos, width = tokens.shape
    length = own_pos * ranks
    total = seqs * length
    own = seqs * own_pos
    rows = w_query.shape[0]
    heads = width // HEAD_DIM
    slots = -(-heads // ranks)
    span = slots * HEAD_DIM
    share = shared_gate.shape[1] // ranks
    names = router.shape[1]
    count = expert_gate.shape[0]

    groups = lax.axis_size("dp")

    def in_order(a):
        return a.reshape(ranks, seqs, own_pos, -1).transpose(1, 0, 2, 3).reshape(total, -1)

    def by_rank(a):
        return a.reshape(seqs, ranks, own_pos, -1).transpose(1, 0, 2, 3).reshape(total, -1)

    def by_share(w):
        return w.reshape(rows, ranks, share).transpose(1, 0, 2)

    def to_all(w):
        return jnp.broadcast_to(w[None], (ranks,) + w.shape)

    pieces = [
        by_share(shared_gate), by_share(shared_up), to_all(router), to_all(attn_gain[:, None]), to_all(ffn_gain[:, None]),
    ]
    edges = [0]
    for p in pieces:
        edges.append(edges[-1] + p.shape[-1])
    pack = jnp.concatenate(pieces, -1)
    pack = jnp.pad(pack, ((0, 0), (0, 0), (0, span - edges[-1])))
    group_x, w_slices = front(
        ranks, groups, heads, slots, tokens.reshape(own, width), w_query, w_key, w_value, pack
    )
    landed = w_slices[3]
    s_gate = landed[:, edges[0] : edges[1]]
    s_up = landed[:, edges[1] : edges[2]]
    full_router = landed[:, edges[2] : edges[3]]
    gain_one = landed[:, edges[3]][None, :]
    gain_two = landed[:, edges[4]][None, :].astype(F32)
    cosine, sine = rotary_tables(length)
    inverse_one, q, k, v, mixed, lse, half_out = attend(
        ranks, groups, seqs, slots, in_order(group_x), gain_one, w_slices[0], w_slices[1], w_slices[2],
        cosine, sine, w_output,
    )

    top = expert_ids.shape[-1]
    extended = jnp.concatenate(
        [
            cotangent.reshape(own, width),
            expert_ids.reshape(own, top).astype(BF),
            jnp.zeros((own, -top % LANES), BF),
        ],
        -1,
    )
    group_c = lax.all_gather(extended, "expert", axis=0, tiled=True)
    group_ids = group_c[:, width : width + top].astype(jnp.int32)

    inputs = tokens.reshape(own, width).astype(F32)
    resid, normed_two, all_mixed, all_out, all_c1 = project(
        ranks, heads, slots, group_x, by_rank(mixed), half_out, gain_two, group_c
    )
    padded_out = jnp.pad(all_out, ((0, slots * ranks * HEAD_DIM - width), (0, 0)))
    w_out = lax.dynamic_index_in_dim(
        padded_out.reshape(slots, ranks, HEAD_DIM, width), me, 1, keepdims=False
    ).reshape(span, width)

    probs = jax.nn.softmax(dot(normed_two, full_router), axis=-1)
    mine = me * count + jnp.arange(count)
    chosen = jnp.any(group_ids[:, :, None] == mine[None, None, :], axis=1).astype(F32)
    weight = chosen * lax.dynamic_slice_in_dim(probs, me * count, count, 1)
    high = weight.astype(BF)
    low = (weight - high.astype(F32)).astype(BF)
    packed = jnp.concatenate([high, low, jnp.zeros((total, LANES - 2 * count), BF)], -1)
    eye = (jnp.arange(names)[None, :] == mine[:, None]).astype(F32)
    layer_part, d_normed_part, d_log, d_s_gate, d_s_up, d_s_down, all_n, all_c2, all_w = experts(
        normed_two, group_c, probs, weight, packed, eye, expert_gate, expert_up, expert_down,
        s_gate, s_up, shared_down, full_router,
    )
    router_part = dot_tn(normed_two, d_log)
    every = ((normed_two, group_c, packed), (all_n, all_c1, all_c2, all_w))
    banks = (expert_gate, expert_up, expert_down)
    hidden = expert_gate.shape[-1]
    cut = hidden * 4 // 7 if hidden % (7 * LANES) == 0 else hidden // 2

    def after(late, *earlier):
        return lax.optimization_barrier((late, earlier))[0]

    def scatter(partial):
        return lax.psum_scatter(partial, "expert", scatter_dimension=0, tiled=True)

    grads = expert_weights(0, 0, cut, every, banks)
    d_normed_two, grads = lax.optimization_barrier((scatter(d_normed_part), grads))
    d_normed_two = d_normed_two.astype(F32)
    inverse_two = lax.rsqrt(jnp.mean(resid * resid, -1, keepdims=True) + EPS)
    ffn_gain_part = jnp.sum(d_normed_two * resid * inverse_two, 0)
    d_out = cotangent.reshape(own, width).astype(F32)
    d_resid = d_out + norm_back(d_normed_two, resid, inverse_two, gain_two)
    own_att = d_resid.astype(BF)
    d_att = lax.all_gather(own_att, "expert", axis=0, tiled=True)
    grads = expert_weights(0, cut, hidden - cut, after(every, own_att), banks, grads)
    d_att, grads = lax.optimization_barrier((d_att, grads))

    d_normed_part, d_wq, d_wk, d_wv, attn_gain_part = attend_back(
        seqs, slots, in_order(d_att), in_order(group_x), inverse_one, gain_one, w_slices[:3], w_out,
        cosine, sine, q, k, v, lse
    )
    d_qkv = jnp.concatenate([d_wq, d_wk, d_wv], -1)
    grads = expert_weights(1, 0, hidden, after(every, attn_gain_part), banks, grads)
    g_gate, g_up, g_down = grads
    d_normed_one = scatter(by_rank(d_normed_part)).astype(F32)
    own_inverse = lax.rsqrt(jnp.mean(inputs * inputs, -1, keepdims=True) + EPS)
    input_grad = d_resid + norm_back(d_normed_one, inputs, own_inverse, gain_one.astype(F32))
    layer_output = resid + scatter(layer_part).astype(F32)
    own_mixed = lax.dynamic_slice_in_dim(all_mixed, me * rows, rows, 1)
    d_wo_rows = dot_tn(own_mixed, d_att).astype(BF)

    def to_rows(g):
        return g.reshape(ranks, rows, -1)

    pieces = [
        to_rows(d_qkv), to_rows(d_s_gate.astype(BF)), to_rows(d_s_up.astype(BF)), to_rows(router_part.astype(BF)),
        to_rows(attn_gain_part.astype(BF)), to_rows(ffn_gain_part.astype(BF)),
    ]
    used = sum(p.shape[-1] for p in pieces)
    packed = jnp.pad(jnp.concatenate(pieces, -1), ((0, 0), (0, 0), (0, -used % LANES)))
    landed = lax.all_to_all(packed, "expert", 0, 0, tiled=True)
    edges = [0]
    for p in pieces:
        edges.append(edges[-1] + p.shape[-1])

    def heads_back(part):
        part = part.reshape(ranks, rows, slots, HEAD_DIM).transpose(1, 2, 0, 3)
        return part.reshape(rows, slots * ranks * HEAD_DIM)[:, :width]

    def shares_back(part):
        return part.transpose(1, 0, 2).reshape(rows, ranks * share)

    def summed(part):
        return jnp.sum(part.astype(F32), 0).astype(BF)

    sums = lax.psum(
        (
            heads_back(landed[:, :, :span]),
            heads_back(landed[:, :, span : 2 * span]),
            heads_back(landed[:, :, 2 * span : 3 * span]),
            d_wo_rows,
            shares_back(landed[:, :, edges[1] : edges[2]]),
            shares_back(landed[:, :, edges[2] : edges[3]]),
            summed(landed[:, :, edges[3] : edges[4]]),
            summed(landed[:, :, edges[4]]),
            summed(landed[:, :, edges[5]]),
            d_s_down.astype(BF),
        ),
        "dp",
    )
    g_q, g_k, g_v, g_o, g_sg, g_su, g_r, g_one, g_two, g_sd = [s.astype(F32) for s in sums]
    return (
        layer_output.astype(BF).reshape(tokens.shape),
        input_grad.astype(BF).reshape(tokens.shape),
        g_one, g_two, g_q, g_k, g_v, g_o, g_r, g_sg, g_su, g_sd, g_gate, g_up, g_down,
    )


def solution(mesh):
    row = P("expert", None)
    experts_spec = P("expert", None, None)
    tokens_spec = P("dp", "expert", None)
    return jax.shard_map(
        body,
        mesh=mesh,
        in_specs=(tokens_spec, tokens_spec, P("expert"), P("expert"))
        + (row,) * 8
        + (experts_spec,) * 3
        + (P(("dp", "expert"), None, None),),
        out_specs=(tokens_spec, tokens_spec, P("expert"), P("expert")) + (row,) * 8 + (experts_spec,) * 3,
        check_vma=False,
    )
```

time: 1990 us -> 674 us (0.34)
  the two profiles are of different devices: /device:TPU:13 before, /device:TPU:0 now
where the time goes in v1:
time: 674 us; the launch traced here: 667 us
  Pallas kernels  445 us (66%)
  waiting for transfers between devices  80.1 us (12%)
  local copies, waits for them, and re-layouts  59.4 us (9%)
  other arithmetic  33.7 us (5%)
  blocking collectives  17 us (3%)
  between operations  15 us (2%)
  starting transfers between devices  9.53 us (1%)
  matrix products  7.58 us (1%)
    pallas_call x3, Pallas kernels, expert_weights(): pl.pallas_call(functools.partial(weights_kernel, j, count, first, size, o...  162 us
    pallas_call x1, Pallas kernels, experts(): pl.pallas_call(functools.partial(experts_kernel, count, steps), grid=(ste...  104 us
    pallas_call x1, Pallas kernels, front(): pl.pallas_call(functools.partial(front_kernel, ranks, groups, heads, slot...  82.4 us
    all_to_all x1, waiting for transfers between devices, body(): landed = lax.all_to_all(packed, 'expert', 0, 0, tiled=True)  79.9 us
    pallas_call x2, Pallas kernels, vmem_call(): pl.pallas_call(kernel, out_shape=outs, in_specs=[spec] * len(args), out_s...  55.3 us
    pallas_call x1, Pallas kernels, project(): pl.pallas_call(functools.partial(project_kernel, ranks, heads, slots), ou...  41.2 us
    psum x1, blocking collectives, body(): lax.psum((heads_back(landed[:, :, :span]), heads_back(landed[:, :, span:2...  17 us
  transfers between devices with their start and end apart: 7, of which 1 were waited for; matrix products, arithmetic and copies ran while one was open for 11% of the time, Pallas kernels for 42%

profile of v1, /device:TPU:0, one launch (start us, length us, event | category | flops | bytes accessed | tf_op | source)
XLA Modules:
  0.0 667.2 jit_solution(9923278376973056175)
XLA Ops:
  8.1 1.8 concatenate.24
  10.8 1.3 reshape.201
  12.1 1.3 reshape.202
  13.8 3.0 concatenate.21
  16.8 1.0 pad.12.pack_ref
  17.8 82.4 %front.1 = (bf16[8,128,1280]{2,1,0:T(8,128)(2,1)}, bf16[4,1280,256]{2,1,0:T(8,128)(2,1)}) custom-call(bf16[128,1280]{1,0:T(8,128)(2,1)} %bitcast.68, bf16[160,1280]{1,0:T(8,128)(2,1)} %wq_ref.1, bf16[160,1280]{1,0:T(8,128)(2,1)} %wk_ref.1, bf16[160,1280]{1,0:T(8,128)(2,1)} %wv_ref.1, bf16[8,160,256]{2,1,0:T(8,128)(2,1)} %pad.12.pack_ref), custom_call_target="tpu_custom_call" | custom-call | tf_op jit(solution)/shard_map/front/pallas_call | solution.py:379
  100.2 3.0 slice_bitcast_fusion
  103.2 0.9 slice.90.router_ref
  105.0 1.0 convert_reduce_fusion
  106.6 1.9 fusion.18
  108.5 1.3 pad_maximum_fusion.1
  109.8 38.0 %attend.1 = (f32[1024,1]{1,0:T(8,128)}, bf16[1024,256]{1,0:T(8,128)(2,1)}, bf16[1024,256]{1,0:T(8,128)(2,1)}, bf16[1024,256]{1,0:T(8,128)(2,1)}, bf16[1024,256]{...) custom-call(bf16[1024,1280]{1,0:T(8,128)(2,1)} %bitcast.63, ...), custom_call_target="tpu_custom_call" | custom-call | tf_op jit(solution)/shard_map/attend/pallas_call | solution.py:53
  148.5 1.0 fusion.24
  149.5 1.0 slice_convert_fusion
  151.1 41.2 %project.1 = (f32[128,1280]{1,0:T(8,128)}, bf16[1024,1280]{1,0:T(8,128)(2,1)}, bf16[1024,1280]{1,0:T(8,128)(2,1)}, bf16[1280,1280]{1,0:T(8,128)(2,1)}, bf16[6,512,640]{2,1,0:T(8,128)(2,1)}) custom-call(bf16[8,128,1280]{2,1,0:T(8,128)(2,1)} %get-tuple-element.74.x_ref, bf16[1024,256]{1,0:T(8,128)(2,1)} %get-tuple-element.76.mixed_ref, ...), custom_call_target="tpu_custom_call" | custom-call | tf_op jit(solution)/shard_map/project/pallas_call | solution.py:483
  192.3 2.6 fusion.25
  195.8 1.0 subtract_convert_fusion
  196.8 0.9 maximum_maximum_fusion.w_group.packed_own
  197.7 104.2 %experts.1 = (bf16[1024,1280]{1,0:T(8,128)(2,1)}, bf16[1024,1280]{1,0:T(8,128)(2,1)}, bf16[1024,16]{1,0:T(8,128)(2,1)}, f32[1280,112]{1,0:T(8,128)}, f32[1280,11...) custom-call(bf16[1024,1280]{1,0:T(8,128)(2,1)} %get-tuple-element.12, ...), custom_call_target="tpu_custom_call" | custom-call | flops 28185722880 | bytes 31457280 | tf_op jit(solution)/shard_map/experts/pallas_call | solution.py:807
  302.0 1.0 copy-done.1
  303.1 42.8 %expert_weights.3 = (f32[2,1280,896]{2,1,0:T(8,128)}, f32[2,1280,896]{2,1,0:T(8,128)}, f32[2,896,1280]{2,1,0:T(8,128)}) custom-call(bf16[1024,1280]{1,0:T(8,128)(2,1)} %get-tuple-element.120.n_ref.n_group.n_own, bf16[1024,1408]{1,0:T(8,128)(2,1)} %all-gather.3.cloned.1.call-done.c_ref.c_group.c_own, ...), custom_call_target="tpu_custom_call" | custom-call | flops 24159191040 | bytes 41943040 | tf_op jit(solution)/shard_map/expert_weights/pallas_call | solution.py:921
  345.9 1.2 fusion.6
  347.2 1.9 fusion.22
  349.2 2.3 pad.13
  351.4 0.9 constant_dynamic-slice_fusion
  352.3 40.1 %expert_weights.4 = (f32[2,1280,896]{2,1,0:T(8,128)}, f32[2,1280,896]{2,1,0:T(8,128)}, f32[2,896,1280]{2,1,0:T(8,128)}) custom-call(bf16[1024,1280]{1,0:T(8,128)(2,1)} %get-tuple-element.120.n_ref.n_group.n_own, bf16[1024,1408]{1,0:T(8,128)(2,1)} %all-gather.3.cloned.1.call-done.c_ref.c_group.c_own, ...), custom_call_target="tpu_custom_call", output_to_operand_aliasing={{0}: (10, {}), {1}: (11, {}), {2}: (12, {})} | custom-call | flops 18119393280 | bytes 41943040 | tf_op jit(solution)/shard_map/expert_weights/pallas_call | solution.py:921
  392.5 17.3 %attend_back.1 = (bf16[1024,1280]{1,0:T(8,128)(2,1)}, bf16[1280,256]{1,0:T(8,128)(2,1)}, bf16[1280,256]{1,0:T(8,128)(2,1)}, bf16[1280,256]{1,0:T(8,128)(2,1)}, f32[1,1280]{1,0:T(1,128)}) custom-call(bf16[1024,1280]{1,0:T(8,128)(2,1)} %all-gather.5.cloned.1.call-done.da_ref, bf16[1024,1280]{1,0:T(8,128)(2,1)} %bitcast.64, ...), custom_call_target="tpu_custom_call" | custom-call | tf_op jit(solution)/shard_map/attend_back/pallas_call | solution.py:53
  409.9 1.7 copy-done
  411.6 1.4 convolution_convert_fusion.1
  413.0 0.9 copy.114
  413.9 1.8 convert_element_type.174
  415.8 1.8 convert_element_type.175
  417.6 1.3 convert_element_type.195
  418.9 1.4 pad_maximum_fusion
  420.4 1.3 reshape.224
  421.7 5.0 concatenate.27
  426.7 2.0 pad.14
  428.7 9.3 %all-to-all-start = ((bf16[8,160,1024]{2,1,0:T(8,128)(2,1)}), bf16[8,160,1024]{2,1,0:T(8,128)(2,1)S(1)}, u32[]{:S(2)}, u32[]{:S(2)}) async-start(bf16[8,160,1024]{2,1,0:T(8,128)(2,1)} %pad.14), calls=%async_computation.3 | async-start | bytes 5242880 | tf_op jit(solution)/shard_map/all_to_all | solution.py:1083
  438.0 1.8 convert_element_type.190
  439.8 3.5 convolution_convert_fusion
  443.4 79.9 %all-to-all-done = bf16[8,160,1024]{2,1,0:T(8,128)(2,1)S(1)} async-done(((bf16[8,160,1024]{2,1,0:T(8,128)(2,1)}), bf16[8,160,1024]{2,1,0:T(8,128)(2,1)S(1)}, u32[]{:S(2)}, u32[]{:S(2)}) %all-to-all-start) | async-done | bytes 2621472 | tf_op jit(solution)/shard_map/all_to_all | solution.py:1083
  523.2 1.4 fusion.23
  524.6 2.5 reshape.217
  527.1 1.9 copy.110
  529.9 0.9 slice_bitcast_fusion.4
  530.8 0.9 copy.112
  531.7 2.0 reshape.220
  533.7 1.8 copy.111
  535.5 2.0 reshape.219
  537.5 2.5 reshape.215
  540.0 1.9 copy.109
  542.8 2.5 reshape.213
  545.4 1.9 copy.108
  548.2 79.0 %expert_weights.5 = (f32[2,1280,896]{2,1,0:T(8,128)}, f32[2,1280,896]{2,1,0:T(8,128)}, f32[2,896,1280]{2,1,0:T(8,128)}) custom-call(bf16[1024,1280]{1,0:T(8,128)(2,1)} %get-tuple-element.120.n_ref.n_group.n_own, bf16[1024,1408]{1,0:T(8,128)(2,1)} %all-gather.3.cloned.1.call-done.c_ref.c_group.c_own, ...), custom_call_target="tpu_custom_call", output_to_operand_aliasing={{0}: (10, {}), {1}: (11, {}), {2}: (12, {})} | custom-call | flops 42278584320 | bytes 41943040 | tf_op jit(solution)/shard_map/expert_weights/pallas_call | solution.py:921
  627.7 17.0 %all-reduce.3 = (bf16[160,16]{1,0:T(8,128)(2,1)S(1)}, bf16[160]{0:T(256)(128)(2,1)S(1)}, bf16[160]{0:T(256)(128)(2,1)S(1)}) all-reduce(bf16[160,16]{1,0:T(8,128)(2,1)S(1)} %slice_reduce_fusion, bf16[160]{0:T(256)(128)(2,1)S(1)} %get-tuple-element.179, ...), channel_id=1, replica_groups=mesh['dp'=4,'expert'=8] {'dp'}, use_global_device_ids=true, to_apply=%region_20.21 | all-reduce | flops 2880 | bytes 11520 | tf_op jit(solution)/shard_map/psum | solution.py:1098
  646.6 1.3 fusion.7
  647.9 2.5 fusion.17
  650.5 2.0 convert_element_type.182
  652.5 1.9 convert_element_type.188
  654.4 1.8 convert_element_type.189
  656.2 0.8 convert_element_type.191
  657.1 0.9 convert_element_type.183
  658.0 0.9 convert_element_type.184
  659.0 0.9 convert_element_type.186
  (86 shorter events, 11.6 us)
Async XLA Ops:
  7.2 6.4 copy-start.13
  7.2 6.5 copy-start.14
  7.2 142.3 %all-gather.3.cloned.1.call-start = ((), (), s32[]{:S(2)}) async-start(), calls=%async_computation.4 | async-start | bytes 3244032 | tf_op jit(solution)/shard_map/all_gather | solution.py:1012
  9.9 336.1 %reduce-scatter.6.cloned.1.call-start = ((), (), s32[]{:S(2)}) async-start(), calls=%async_computation.6 | async-start | bytes 2949120 | tf_op jit(solution)/shard_map/reduce_scatter | solution.py:1046
  195.8 1.9 copy-start.3
  301.9 1.1 copy-start.1
  301.9 90.6 %all-gather.5.cloned.1.call-start = ((), (), s32[]{:S(2)}) async-start(), calls=%async_computation.7 | async-start | bytes 2949120 | tf_op jit(solution)/shard_map/all_gather | solution.py:1056
  303.1 44.0 %copy-start.2 = (bf16[1,128,1280]{2,1,0:T(8,128)(2,1)S(1)}, bf16[1,128,1280]{2,1,0:T(8,128)(2,1)}, u32[]{:S(2)}) copy-start(bf16[1,128,1280]{2,1,0:T(8,128)(2,1)} %param.17) | copy-start | bytes 983044
  349.1 297.5 %reduce-scatter.8.cloned.1.call-start = ((), (), s32[]{:S(2)}) async-start(), calls=%async_computation.8 | async-start | bytes 2949120 | tf_op jit(solution)/shard_map/reduce_scatter | solution.py:1046
  409.8 1.7 copy-start
  409.8 238.1 %reduce-scatter.4.cloned.1.call-start = ((), (), s32[]{:S(2)}) async-start(), calls=%async_computation.5 | async-start | bytes 2949120 | tf_op jit(solution)/shard_map/reduce_scatter | solution.py:1046
  413.0 6.0 copy-start.4
  413.0 6.0 copy-start.5
  413.0 6.0 copy-start.6
  417.6 2.7 copy-start.12
  428.7 94.6 %all-to-all-start = ((bf16[8,160,1024]{2,1,0:T(8,128)(2,1)}), bf16[8,160,1024]{2,1,0:T(8,128)(2,1)S(1)}, u32[]{:S(2)}, u32[]{:S(2)}) async-start(bf16[8,160,1024]{2,1,0:T(8,128)(2,1)} %pad.14), calls=%async_computation.3 | async-start | bytes 5242880 | tf_op jit(solution)/shard_map/all_to_all | solution.py:1083
  438.0 212.5 %all-reduce.7.cloned.1.call-start = ((), (), s32[]{:S(2)}) async-start(), calls=%async_computation.9 | async-start | bytes 4997120 | tf_op jit(solution)/shard_map/psum | solution.py:1098
  548.2 98.4 %copy-start.11 = (f32[1280]{0:T(1024)S(1)}, f32[1280]{0:T(1024)}, u32[]{:S(2)}) copy-start(f32[1280]{0:T(1024)} %get-tuple-element.182) | copy-start | bytes 15364
  650.5 5.7 copy-start.10
  650.5 6.6 copy-start.9
  650.5 7.5 %copy-start.8 = (bf16[160,1280]{1,0:T(8,128)(2,1)S(1)}, bf16[160,1280]{1,0:T(8,128)(2,1)}, u32[]{:S(2)}) copy-start(bf16[160,1280]{1,0:T(8,128)(2,1)} %get-tuple-element.191) | copy-start | bytes 1228804
  652.5 6.4 copy-start.7
Sparse Core Ops, SparseCore 0:
  10.2 54.7 all-gather.2
  302.1 41.9 reduce-scatter.5
  349.2 38.3 all-gather.4
  410.0 47.9 reduce-scatter.7
  460.1 68.6 reduce-scatter.3
  548.3 77.8 all-reduce.6

commit v2 on v1

--- a/solution.py
+++ b/solution.py
@@ -212,7 +212,11 @@
         return self.copy(6 + 2 * slot + j, self.piece(slot, j), self.piece(slot + 3, j), expert=self.twin)
 
     def start(self):
-        for k in range(4):
+        for k in range(2):
+            self.direct(k).start()
+
+    def more(self):
+        for k in range(2, 4):
             self.direct(k).start()
 
     def relay(self):
@@ -268,7 +272,7 @@
     def relay(self):
         pass
 
-    hand_over = relay
+    hand_over = more = relay
 
     def finish(self):
         for k in range(3):
@@ -276,24 +280,27 @@
                 self.copy(k, h).wait()
 
 
+def head_of(s, i, ranks):
+    return i if s == 0 else s * ranks + i // 2 + (i % 2) * (ranks // 2)
+
+
 def aligned(i, size):
     return pl.ds(pl.multiple_of(i * size, size), size)
 
 
 def front_kernel(
-    ranks, groups, heads, slots, x_ref, wq_ref, wk_ref, wv_ref, pack_ref,
-    gx_ref, w_ref, stage_ref, land_ref,
-    x_send, x_recv, w_send, w_recv, d_send, d_recv,
+    ranks, groups, heads, slots, x_ref, c_ref, wq_ref, wk_ref, wv_ref, pack_ref, wo_ref,
+    gx_ref, gc_ref, wqs_ref, wks_ref, wvs_ref, wps_ref, small_ref, half_ref, stage_ref, land_ref, ostage_ref,
+    x_send, x_recv, c_send, c_recv, w_send, w_recv, d_send, d_recv, o_send, o_recv, p_send, p_recv,
 ):
     me, g = lax.axis_index("expert"), lax.axis_index("dp")
-    rows = wq_ref.shape[0]
+    rows, width = wq_ref.shape
+    units = width // LANES
+    per = ostage_ref.shape[0]
     peers = [lax.rem(g + d, groups) for d in range(1, groups)]
     others = [lax.rem(me + d, ranks) for d in range(1, ranks)]
     meet([{"expert": t} for t in others] + [{"dp": t} for t in peers])
 
-    tokens = LineGather(ranks, x_ref, lambda i: gx_ref.at[i], x_send, x_recv)
-    tokens.start()
-
     def stage_heads(w):
         for u in range(heads):
             stage_ref[u] = w[:, u * LANES : (u + 1) * LANES]
@@ -303,12 +310,13 @@
 
     def stage_pack():
         for s in range(slots):
-            stage_ref[pl.ds(s * ranks, ranks)] = pack_ref[:, :, s * LANES : (s + 1) * LANES]
+            for t in range(ranks):
+                stage_ref[head_of(s, t, ranks)] = pack_ref[t, :, s * LANES : (s + 1) * LANES]
 
     pl.when(g == groups - 1)(stage_pack)
 
     def known(s, t, group=None):
-        return jnp.logical_or((g if group is None else group) == groups - 1, s * ranks + t < heads)
+        return jnp.logical_or((g if group is None else group) == groups - 1, head_of(s, t, ranks) < heads)
 
     def weight_copy(s, d, unit, i, to):
         return remote(
@@ -318,19 +326,35 @@
     for d in range(1, ranks):
         t = others[d - 1]
         for s in range(slots):
-            guarded(known(s, t), lambda: weight_copy(s, d, s * ranks + t, me, t).start())
+            guarded(known(s, t), lambda: weight_copy(s, d, head_of(s, t, ranks), me, t).start())
+
+    def stage_out(which):
+        for k in range(per):
+            u = which * per + k
+            if u < units:
+                ostage_ref[k] = wo_ref[:, u * LANES : (u + 1) * LANES]
+
+    for which in range(groups):
+        pl.when(g == which)(functools.partial(stage_out, which))
+    out_rows = LineGather(
+        ranks, ostage_ref, lambda i: half_ref.at[g, :, i // 2], o_send, o_recv, twins=False
+    )
+    out_rows.start()
+    tokens = LineGather(ranks, x_ref, lambda i: gx_ref.at[i], x_send, x_recv)
+    tokens.start()
+    half_ref[g, :, me // 2] = ostage_ref[...]
     for s in range(slots):
         def keep(s=s):
-            land_ref[g, s, me] = stage_ref[s * ranks + me]
+            land_ref[g, s, me] = stage_ref[head_of(s, me, ranks)]
 
         pl.when(known(s, me))(keep)
         for which in range(groups - 1):
             def clear(s=s, which=which):
                 land_ref[which, s] = jnp.zeros(land_ref.shape[2:], BF)
 
-            pl.when(s * ranks + me >= heads)(clear)
-
+            pl.when(head_of(s, me, ranks) >= heads)(clear)
     gx_ref[me] = x_ref[...]
+    gc_ref[me] = c_ref[...]
 
     def share(s, part, d, to):
         return remote(part, part, d_send.at[s, d], d_recv.at[s, d], dp=to)
@@ -341,19 +365,39 @@
             for d in range(1, groups):
                 pl.when(known(s, me))(lambda: share(s, part, d, peers[d - 1]).start())
 
+    def out_share(d, k, group):
+        part = half_ref.at[group, k]
+        return remote(part, part, p_send.at[d, k], p_recv.at[d, k], dp=peers[d - 1])
+
+    def held(group, k):
+        return True if (groups - 1) * per + k < units else group * per + k < units
+
     pass_on(me)
+    for d in range(1, ranks):
+        i = lax.rem(me + ranks - d, ranks)
+        for s in range(slots):
+            pl.when(known(s, me))(lambda: weight_copy(s, d, 0, i, others[0]).wait_recv())
+        pass_on(i)
     steps = ranks // 2 - 1
-    taken = 1
     for step in range(1, steps + 1):
+        out_rows.step(step)
+        if step == 1:
+            tokens.step(1)
+    out_rows.finish()
+    for d in range(1, groups):
+        for k in range(per):
+            guarded(held(g, k), out_share(d, k, g).start)
+    cots = LineGather(ranks, c_ref, lambda i: gc_ref.at[i], c_send, c_recv)
+    for step in range(2, steps + 1):
         tokens.step(step)
-        until = ranks if step == steps else min(ranks, taken + 2)
-        for d in range(taken, until):
-            i = lax.rem(me + ranks - d, ranks)
-            for s in range(slots):
-                pl.when(known(s, me))(lambda: weight_copy(s, d, 0, i, others[0]).wait_recv())
-            pass_on(i)
-        taken = until
+        if step == steps - 1:
+            cots.start()
+    if steps < 3:
+        cots.start()
+    for step in range(1, steps + 1):
+        cots.step(step)
     tokens.finish()
+    cots.finish()
     for d in range(1, ranks):
         t = others[d - 1]
         for s in range(slots):
@@ -363,96 +407,125 @@
         for s in range(slots):
             pl.when(known(s, me))(lambda: share(s, land_ref.at[g, s], d, peers[d - 1]).wait_send())
             pl.when(known(s, me, there))(lambda: share(s, land_ref.at[there, s], d, peers[d - 1]).wait_recv())
-    for which in range(groups):
+        for k in range(per):
+            guarded(held(g, k), out_share(d, k, g).wait_send)
+            guarded(held(there, k), out_share(d, k, there).wait_recv)
+    for which, ref in enumerate((wqs_ref, wks_ref, wvs_ref, wps_ref)):
         for s in range(slots):
             for r in range(ranks):
-                w_ref[which, r * rows : (r + 1) * rows, s * LANES : (s + 1) * LANES] = land_ref[which, s, r]
-
-
-def front(ranks, groups, heads, slots, x, w_query, w_key, w_value, pack):
+                ref[r * rows : (r + 1) * rows, s * LANES : (s + 1) * LANES] = land_ref[which, s, r]
+    small_ref[...] = jnp.transpose(wps_ref[:, (slots - 1) * LANES :].astype(F32))
+
+
+def front(ranks, groups, heads, slots, x, cot, w_query, w_key, w_value, pack, w_output):
     own, width = x.shape
     rows = w_query.shape[0]
+    per = -(-(width // LANES) // groups)
     line = LineGather.semaphores(ranks)
     dma = pltpu.SemaphoreType.DMA
     spec = pl.BlockSpec(memory_space=pltpu.VMEM)
     shape = jax.ShapeDtypeStruct
     return pl.pallas_call(
         functools.partial(front_kernel, ranks, groups, heads, slots),
-        out_shape=[
-            shape((ranks, own, width), BF),
-            shape((groups, width, slots * LANES), BF),
-        ],
-        in_specs=[spec] * 5,
-        out_specs=[spec] * 2,
+        out_shape=[shape((ranks, own, width), BF), shape((ranks,) + cot.shape, BF)]
+        + [shape((width, slots * LANES), BF)] * 4
+        + [shape((LANES, width), F32), shape((groups, per, ranks // 2, rows, LANES), BF)],
+        in_specs=[spec] * 7,
+        out_specs=[spec] * 8,
         scratch_shapes=[
             pltpu.VMEM((slots * ranks, rows, LANES), BF),
             pltpu.VMEM((groups, slots, ranks, rows, LANES), BF),
+            pltpu.VMEM((per, rows, LANES), BF),
+            dma((line,)), dma((line,)),
             dma((line,)), dma((line,)),
             dma((slots, ranks)), dma((slots, ranks)),
             dma((slots, groups)), dma((slots, groups)),
+            dma((line,)), dma((line,)),
+            dma((groups, per)), dma((groups, per)),
         ],
         compiler_params=pltpu.CompilerParams(
             collective_id=0, has_side_effects=True, vmem_limit_bytes=VMEM_LIMIT
         ),
         name="front",
-    )(x, w_query, w_key, w_value, pack)
+    )(x, cot, w_query, w_key, w_value, pack, w_output)
 
 
 def project_kernel(
-    ranks, heads, slots, x_ref, mixed_ref, half_ref, gain_ref, c_ref,
-    resid_ref, n_ref, all_ref, wo_ref, c_all_ref, other_ref, send, recv, t_send, t_recv, a_send, a_recv,
+    ranks, groups, heads, slots, count, top, route_at,
+    first, x_ref, mixed_ref, half_ref, small_ref, pack_ref, c_ref,
+    resid_ref, n_ref, all_ref, wo_ref, packed_ref, c_all_ref, other_ref, id_ref,
+    send, recv, t_send, t_recv, a_send, a_recv, load,
 ):
-    me = lax.axis_index("expert")
+    me, g = lax.axis_index("expert"), lax.axis_index("dp")
     chips = ranks // 2
     z = me // 2
-    share = c_all_ref.shape[-1]
-    across = Across(lambda r: c_ref.at[r, pl.ds(0, share)], c_all_ref, a_send, a_recv)
-    meet_near(chips, z, me, [across.by_x, across.by_y])
     twin = me + 1 - 2 * lax.rem(me, 2)
-    halves = remote(half_ref, other_ref, t_send, t_recv, expert=twin)
-    halves.start()
-    across.start()
+    per, part = half_ref.shape[1], half_ref.shape[3]
+    units = wo_ref.shape[1] // LANES
+    peers = [lax.rem(g + d, groups) for d in range(1, groups)]
+    lanes = c_all_ref.shape[-1]
+    across = Across(lambda r: c_ref.at[r, pl.ds(first, lanes)], c_all_ref, a_send, a_recv)
+    meet_near(chips, z, me, peers)
+    ids = pltpu.make_async_copy(c_ref.at[:, pl.ds(wo_ref.shape[1], LANES)], id_ref, load)
+    ids.start()
     line = LineGather.semaphores(ranks)
     parts = []
     for s in range(slots):
         def head(i, s=s):
-            return aligned(jnp.clip(s * ranks + i, 0, heads - 1), LANES)
+            return aligned(jnp.clip(head_of(s, i, ranks), 0, heads - 1), LANES)
 
         cols = slice(s * LANES, (s + 1) * LANES)
-        ok = (lambda i: True) if (s + 1) * ranks <= heads else (lambda i, s=s: s * ranks + i < heads)
+        ok = (lambda i: True) if (s + 1) * ranks <= heads else (lambda i, s=s: head_of(s, i, ranks) < heads)
         gather = LineGather(
             ranks, mixed_ref.at[:, cols], lambda i, head=head: all_ref.at[:, head(i)], send, recv, s * line, ok
         )
         gather.start()
         parts.append(gather)
 
-        def keep(cols=cols, head=head):
-            all_ref[:, head(me)] = mixed_ref[:, cols]
-
-        guarded(ok(me), keep)
+    across.start()
+    across.more()
+    for s, gather in enumerate(parts):
+        def keep(s=s):
+            cols = slice(s * LANES, (s + 1) * LANES)
+            all_ref[:, aligned(jnp.clip(head_of(s, me, ranks), 0, heads - 1), LANES)] = mixed_ref[:, cols]
+
+        guarded(gather.valid(me), keep)
+
+    def share_twin(group, k):
+        src = half_ref.at[group, k]
+        return remote(src, other_ref.at[group, k], t_send.at[group, k], t_recv.at[group, k], expert=twin)
+
+    def each_unit(action):
+        for group in range(groups):
+            for k in range(per):
+                if group * per + k < units:
+                    action(share_twin(group, k))
+
+    each_unit(lambda copy: copy.start())
+    middle = (chips + 1) // 2
     for step in range(1, chips):
         for gather in parts:
             gather.step(step)
+        if step == middle:
+            across.relay()
     for gather in parts:
         gather.finish()
-    across.relay()
-    halves.wait()
-    groups, per, _, part, _ = half_ref.shape
+    each_unit(lambda copy: copy.wait())
+    ids.wait()
 
     def lay_out(even, odd):
-        for which in range(groups):
-            for k in range(per):
-                u = which * per + k
-                if u < wo_ref.shape[1] // LANES:
-                    cols = slice(u * LANES, (u + 1) * LANES)
-                    for c in range(chips):
-                        wo_ref[2 * c * part : (2 * c + 1) * part, cols] = even[which, k, c]
-                        wo_ref[(2 * c + 1) * part : (2 * c + 2) * part, cols] = odd[which, k, c]
+        for u in range(units):
+            cols = slice(u * LANES, (u + 1) * LANES)
+            for c in range(chips):
+                wo_ref[2 * c * part : (2 * c + 1) * part, cols] = even[u // per, u % per, c]
+                wo_ref[(2 * c + 1) * part : (2 * c + 2) * part, cols] = odd[u // per, u % per, c]
 
     pl.when(me == 2 * z)(lambda: lay_out(half_ref, other_ref))
     pl.when(me != 2 * z)(lambda: lay_out(other_ref, half_ref))
     blocks, own, width = x_ref.shape
-    gain = gain_ref[...]
+    names = ranks * count
+    gain_at = route_at + names + 1 - (slots - 1) * LANES
+    gain = small_ref[gain_at : gain_at + 1, :]
     tile = 2 if own <= 128 and blocks % 2 == 0 else 1
 
     def rows_of(b):
@@ -460,98 +533,93 @@
         x = x_ref[pl.ds(b * tile, tile)].reshape(tile * own, width).astype(F32)
         resid = x + dot(all_ref[rows, :], wo_ref[...])
         inverse = lax.rsqrt(jnp.mean(resid * resid, -1, keepdims=True) + EPS)
-        n_ref[rows, :] = (resid * inverse * gain).astype(BF)
+        normed = (resid * inverse * gain).astype(BF)
+        n_ref[rows, :] = normed
         for t in range(tile):
             def keep(t=t):
                 resid_ref[...] = resid[t * own : (t + 1) * own]
 
             pl.when(b * tile + t == me)(keep)
-
-    lax.fori_loop(0, blocks // tile, lambda b, c: (rows_of(b), c)[1], 0)
+        probs = route_probs(dot(normed, pack_ref[...]), route_at, names)
+        routes = id_ref[rows, :].astype(jnp.int32)
+        lane = lax.broadcasted_iota(jnp.int32, routes.shape, 1)
+        out = jnp.zeros((tile * own, LANES), F32)
+        for j in range(count):
+            mine = me * count + j
+            chosen = jnp.max(jnp.where((routes == mine) & (lane < top), 1.0, 0.0), -1, keepdims=True)
+            names_at = lax.broadcasted_iota(jnp.int32, probs.shape, 1)
+            weight = chosen * jnp.sum(jnp.where(names_at == mine, probs, 0.0), -1, keepdims=True)
+            high = weight.astype(BF).astype(F32)
+            out = jnp.where(lane == j, high, out)
+            out = jnp.where(lane == count + j, weight - high, out)
+        packed_ref[rows, :] = out.astype(BF)
+
+    half = blocks // tile // 2
+    lax.fori_loop(0, half, lambda b, c: (rows_of(b), c)[1], 0)
     across.hand_over()
+    lax.fori_loop(half, blocks // tile, lambda b, c: (rows_of(b), c)[1], 0)
     across.finish()
 
 
-def project(ranks, heads, slots, x, mixed, half, gain, cot):
+def route_probs(products, first, names):
+    logits = products[:, first : first + names]
+    raised = jnp.exp(logits - jnp.max(logits, -1, keepdims=True))
+    return raised / jnp.sum(raised, -1, keepdims=True)
+
+
+def project(ranks, groups, heads, slots, count, top, route_at, first, lanes, x, mixed, half, small, pack, cot):
     blocks, own, width = x.shape
     total = blocks * own
     line = LineGather.semaphores(ranks)
+    per = half.shape[1]
     dma = pltpu.SemaphoreType.DMA
     spec = pl.BlockSpec(memory_space=pltpu.VMEM)
     anywhere = pl.BlockSpec(memory_space=pl.ANY)
     shape = jax.ShapeDtypeStruct
     return pl.pallas_call(
-        functools.partial(project_kernel, ranks, heads, slots),
+        functools.partial(project_kernel, ranks, groups, heads, slots, count, top, route_at, first),
         out_shape=[
             shape((own, width), F32),
             shape((total, width), BF),
             shape((total, width), BF),
             shape((width, width), BF),
-            shape((6, total // 2, width // 2), BF),
+            shape((total, LANES), BF),
+            shape((6, total // 2, lanes), BF),
         ],
-        in_specs=[spec] * 4 + [anywhere],
-        out_specs=[spec] * 4 + [anywhere],
+        in_specs=[spec] * 5 + [anywhere],
+        out_specs=[spec] * 5 + [anywhere],
         scratch_shapes=[
-            pltpu.VMEM(half.shape, BF), dma((slots * line,)), dma((slots * line,)), dma(()), dma(()),
-            dma((Across.SEMAPHORES,)), dma((Across.SEMAPHORES,)),
+            pltpu.VMEM(half.shape, BF), pltpu.VMEM((total, LANES), BF),
+            dma((slots * line,)), dma((slots * line,)),
+            dma((groups, per)), dma((groups, per)),
+            dma((Across.SEMAPHORES,)), dma((Across.SEMAPHORES,)), dma(()),
         ],
         compiler_params=pltpu.CompilerParams(
-            collective_id=2, has_side_effects=True, vmem_limit_bytes=VMEM_LIMIT
+            collective_id=1, has_side_effects=True, vmem_limit_bytes=VMEM_LIMIT
         ),
         name="project",
-    )(x, mixed, half, gain, cot)
+    )(x, mixed, half, small, pack, cot)
 
 
 def attend_kernel(
-    ranks, groups, seqs, slots, x_ref, gain_ref, wq_ref, wk_ref, wv_ref, cos_ref, sin_ref, wo_ref,
-    inv_ref, q_ref, k_ref, v_ref, mixed_ref, lse_ref, half_ref,
-    stage_ref, o_send, o_recv, p_send, p_recv,
+    seqs, slots, gain_at, x_ref, small_ref, wq_ref, wk_ref, wv_ref, cos_ref, sin_ref, c_ref,
+    inv_ref, q_ref, k_ref, v_ref, mixed_ref, lse_ref, c_all_ref, a_send, a_recv,
 ):
     total, width = x_ref.shape
     length = total // seqs
     block = row_block(length)
     scale = HEAD_DIM ** (-0.5)
-
-    me, g = lax.axis_index("expert"), lax.axis_index("dp")
-    chips, per = half_ref.shape[2], half_ref.shape[1]
-    z = me // 2
-    peers = [lax.rem(g + d, groups) for d in range(1, groups)]
-    meet_near(chips, z, me, peers)
-    for which in range(groups):
-
-        def stage(which=which):
-            for k in range(per):
-                u = which * per + k
-                if u < width // LANES:
-                    stage_ref[k] = wo_ref[:, u * LANES : (u + 1) * LANES]
-
-        pl.when(g == which)(stage)
-    out_rows = LineGather(
-        ranks, stage_ref, lambda i: half_ref.at[g, :, i // 2], o_send, o_recv, twins=False
-    )
-    out_rows.start()
-    half_ref[g, :, z] = stage_ref[...]
-
-    def out_share(d, group, to):
-        part = half_ref.at[group]
-        return remote(part, part, p_send.at[d], p_recv.at[d], dp=to)
-
-    pending = list(range(1, chips))
-
-    def progress():
-        if pending:
-            out_rows.step(pending.pop(0))
-            if not pending:
-                out_rows.finish()
-                for d in range(1, groups):
-                    out_share(d, g, peers[d - 1]).start()
-
+    gain = small_ref[gain_at : gain_at + 1, :]
+    across = Across(lambda r: c_ref.at[r, pl.ds(0, c_all_ref.shape[-1])], c_all_ref, a_send, a_recv)
+    meet(across.peers())
+    across.start()
+    across.more()
     for s in range(seqs):
         for i in range(length // block):
             rows = pl.ds(s * length + i * block, block)
             x = x_ref[rows, :].astype(F32)
             inv = lax.rsqrt(jnp.mean(x * x, -1, keepdims=True) + EPS)
-            normed = (x * inv * gain_ref[...].astype(F32)).astype(BF)
+            normed = (x * inv * gain).astype(BF)
             inv_ref[rows, :] = inv
             cosine = cos_ref[pl.ds(i * block, block), :]
             sine = sin_ref[pl.ds(i * block, block), :]
@@ -562,11 +630,11 @@
                 q_ref[rows, cols] = (q * cosine + pltpu.roll(q, HEAD_DIM // 2, 1) * sine).astype(BF)
                 k_ref[rows, cols] = (k * cosine + pltpu.roll(k, HEAD_DIM // 2, 1) * sine).astype(BF)
             v_ref[rows, :] = valued.astype(BF)
-    progress()
+    across.relay()
     for s in range(seqs):
         for i in range(length // block):
-            if i:
-                progress()
+            if s == 0 and i == length // block - 1:
+                across.hand_over()
             rows = pl.ds(s * length + i * block, block)
             keys = pl.ds(s * length, (i + 1) * block)
             shape = (block, (i + 1) * block)
@@ -584,47 +652,41 @@
                 probs = (raised / totals).astype(BF)
                 mixed_ref[rows, cols] = dot(probs, v_ref[keys, cols]).astype(BF)
                 lse_ref[rows, h : h + 1] = top + jnp.log(totals)
-    while pending:
-        progress()
-    for d in range(1, groups):
-        out_share(d, g, peers[d - 1]).wait_send()
-        out_share(d, lax.rem(g + groups - d, groups), peers[d - 1]).wait_recv()
-
-
-def attend(ranks, groups, seqs, slots, x, gain, w_q, w_k, w_v, cosine, sine, w_output):
+    across.finish()
+
+
+def attend(seqs, slots, gain_at, lanes, x, small, w_q, w_k, w_v, cosine, sine, cot):
     total, width = x.shape
     span = slots * HEAD_DIM
-    rows = w_output.shape[0]
-    per = -(-(width // LANES) // groups)
-    line = LineGather.semaphores(ranks)
+    shape = jax.ShapeDtypeStruct
     dma = pltpu.SemaphoreType.DMA
-    shape = jax.ShapeDtypeStruct
-    return vmem_call(
-        functools.partial(attend_kernel, ranks, groups, seqs, slots),
-        [
+    vmem, anywhere = pl.BlockSpec(memory_space=pltpu.VMEM), pl.BlockSpec(memory_space=pl.ANY)
+    return pl.pallas_call(
+        functools.partial(attend_kernel, seqs, slots, gain_at),
+        out_shape=[
             shape((total, 1), F32),
             shape((total, span), BF),
             shape((total, span), BF),
             shape((total, span), BF),
             shape((total, span), BF),
             shape((total, slots), F32),
-            shape((groups, per, ranks // 2, rows, LANES), BF),
+            shape((6, total // 2, lanes), BF),
         ],
-        x, gain, w_q, w_k, w_v, cosine, sine, w_output,
-        scratch_shapes=[
-            pltpu.VMEM((per, rows, LANES), BF),
-            dma((line,)), dma((line,)),
-            dma((groups,)), dma((groups,)),
-        ],
-        remote_id=1,
+        in_specs=[vmem] * 7 + [anywhere],
+        out_specs=[vmem] * 6 + [anywhere],
+        scratch_shapes=[dma((Across.SEMAPHORES,)), dma((Across.SEMAPHORES,))],
+        compiler_params=pltpu.CompilerParams(
+            collective_id=2, has_side_effects=True, vmem_limit_bytes=VMEM_LIMIT
+        ),
         name="attend",
-    )
+    )(x, small, w_q, w_k, w_v, cosine, sine, cot)
 
 
 def attend_back_kernel(
-    seqs, slots, da_ref, x_ref, inv_ref, g_ref, wq_ref, wk_ref, wv_ref, wo_ref, cos_ref, sin_ref,
+    ranks, heads, seqs, slots, gain_at, da_ref, x_ref, inv_ref, small_ref, wq_ref, wk_ref, wv_ref, wall_ref,
+    cos_ref, sin_ref,
     q_ref, k_ref, v_ref, lse_ref,
-    dn_ref, dwq_ref, dwk_ref, dwv_ref, gain_ref, dmix_ref, dqkv_ref, dk_ref, dv_ref,
+    dn_ref, dwq_ref, dwk_ref, dwv_ref, gain_ref, dmix_ref, dqkv_ref, dk_ref, dv_ref, wo_ref,
 ):
     total, width = da_ref.shape
     length = total // seqs
@@ -632,6 +694,12 @@
     count = length // block
     scale = HEAD_DIM ** (-0.5)
     span = slots * HEAD_DIM
+    me = lax.axis_index("expert")
+    for h in range(slots):
+        cols = slice(h * HEAD_DIM, (h + 1) * HEAD_DIM)
+        head = head_of(h, me, ranks)
+        rows_here = wall_ref[aligned(jnp.minimum(head, heads - 1), HEAD_DIM), :]
+        wo_ref[cols, :] = jnp.where(head < heads, rows_here, jnp.zeros_like(rows_here))
     for s in range(seqs):
         for i in range(count):
             rows = pl.ds(s * length + i * block, block)
@@ -684,42 +752,45 @@
     step = LANES * 2
     for i in range(width // step):
         cols = slice(i * step, (i + 1) * step)
-        normed = (x_ref[:, cols].astype(F32) * inv_ref[...] * g_ref[:, cols].astype(F32)).astype(BF)
+        normed = (x_ref[:, cols].astype(F32) * inv_ref[...] * small_ref[gain_at : gain_at + 1, cols]).astype(BF)
         grads = dot_tn(normed, dqkv_ref[...]).astype(BF)
         dwq_ref[cols, :] = grads[:, :span]
         dwk_ref[cols, :] = grads[:, span : 2 * span]
         dwv_ref[cols, :] = grads[:, 2 * span :]
 
 
-def attend_back(seqs, slots, d_att, x, inverse, gain, w_slices, w_out, cosine, sine, q, k, v, lse):
+def attend_back(ranks, heads, seqs, slots, gain_at, d_att, x, inverse, small, w_slices, w_all, cosine, sine, q, k, v, lse):
     total, width = d_att.shape
     span = slots * HEAD_DIM
     shape = jax.ShapeDtypeStruct
     return vmem_call(
-        functools.partial(attend_back_kernel, seqs, slots),
+        functools.partial(attend_back_kernel, ranks, heads, seqs, slots, gain_at),
         [shape((total, width), BF)] + [shape((width, span), BF)] * 3 + [shape((1, width), F32)],
-        d_att, x, inverse, gain, *w_slices, w_out, cosine, sine, q, k, v, lse,
+        d_att, x, inverse, small, *w_slices, w_all, cosine, sine, q, k, v, lse,
         scratch_shapes=[
             pltpu.VMEM((total, span), BF),
             pltpu.VMEM((total, 3 * span), BF),
             pltpu.VMEM((total // seqs, HEAD_DIM), F32),
             pltpu.VMEM((total // seqs, HEAD_DIM), F32),
+            pltpu.VMEM((span, width), BF),
         ],
         name="attend_back",
     )
 
 
 def experts_kernel(
-    experts, steps, n_ref, c_ref, prob_ref, weight_ref, eye_ref, wg_ref, wu_ref, wd_ref, sg_ref, su_ref, sd_ref,
-    router_ref, n_group, c_group, w_group,
-    out_ref, dx_ref, dlog_ref, dsg_ref, dsu_ref, dsd_ref, n_all, c_all, w_all, send, recv,
+    ranks, count, steps, share, n_ref, c_ref, packed_ref, wg_ref, wu_ref, wd_ref, pack_ref, sd_ref,
+    n_group, c_group, w_group,
+    out_ref, dx_ref, dpack_ref, dsd_ref, n_all, c_all, w_all, send, recv,
 ):
     step = pl.program_id(0)
+    me = lax.axis_index("expert")
+    names = ranks * count
     part = c_all.shape[-1]
     moves = [
+        SameExperts(w_group, w_all, send.at[1], recv.at[1]),
         Across(lambda r: n_group.at[r], n_all, send.at[0], recv.at[0]),
-        SameExperts(w_group, w_all, send.at[1], recv.at[1]),
-        Across(lambda r: c_group.at[r, pl.ds(part, part)], c_all, send.at[2], recv.at[2]),
+        Across(lambda r: c_group.at[r, pl.ds(n_ref.shape[1] - part, part)], c_all, send.at[2], recv.at[2]),
     ]
 
     @pl.when(step == 0)
@@ -728,12 +799,17 @@
         for move in moves:
             move.start()
 
-    @pl.when(step == steps // 3)
+    @pl.when(step == min(1, steps - 1))
+    def _():
+        for move in moves:
+            move.more()
+
+    @pl.when(step == steps // 2)
     def _():
         for move in moves:
             move.relay()
 
-    @pl.when(step == 2 * steps // 3)
+    @pl.when(step == steps - 1)
     def _():
         for move in moves:
             move.hand_over()
@@ -741,40 +817,40 @@
     n = n_ref[...]
     c_b = c_ref[...]
     c = c_b.astype(F32)
-    gate = dot(n, sg_ref[...])
-    up = dot(n, su_ref[...])
+    products = dot(n, pack_ref[...])
+    gate, up = products[:, :share], products[:, share : 2 * share]
     hidden = (silu(gate) * up).astype(BF)
     out = dot(hidden, sd_ref[...])
-    d_gate, d_up = swiglu_back(dot_nt(c_b, sd_ref[...]), gate, up)
-    dx = dot_nt(d_gate, sg_ref[...]) + dot_nt(d_up, su_ref[...])
+    d_gate_s, d_up_s = swiglu_back(dot_nt(c_b, sd_ref[...]), gate, up)
 
     @pl.when(step == 0)
     def _():
-        dsg_ref[...] = jnp.zeros_like(dsg_ref)
-        dsu_ref[...] = jnp.zeros_like(dsu_ref)
+        dpack_ref[...] = jnp.zeros_like(dpack_ref)
         dsd_ref[...] = jnp.zeros_like(dsd_ref)
 
-    dsg_ref[...] += dot_tn(n, d_gate)
-    dsu_ref[...] += dot_tn(n, d_up)
     dsd_ref[...] += dot_tn(hidden, c_b)
-    probs = prob_ref[...]
+    probs = route_probs(products, 2 * share, names)
+    name = lax.broadcasted_iota(jnp.int32, probs.shape, 1)
     d_log = jnp.zeros_like(probs)
     inner = jnp.zeros((n.shape[0], 1), F32)
-    for j in range(experts):
-        weight = weight_ref[:, j : j + 1]
+    dx = jnp.zeros(c.shape, F32)
+    for j in range(count):
+        weight = packed_ref[:, j : j + 1].astype(F32) + packed_ref[:, count + j : count + j + 1].astype(F32)
         gate = dot(n, wg_ref[j])
         up = dot(n, wu_ref[j])
         hidden = (silu(gate) * up).astype(BF)
         y = dot(hidden, wd_ref[j]).astype(BF).astype(F32)
         out += weight * y
         d_weight = weight * jnp.sum(c * y, -1, keepdims=True)
-        d_log += eye_ref[j : j + 1, :] * d_weight
+        d_log += jnp.where(name == me * count + j, d_weight, 0.0)
         inner += d_weight
         d_gate, d_up = swiglu_back(dot_nt((weight * c).astype(BF), wd_ref[j]), gate, up)
         dx += dot_nt(d_gate, wg_ref[j]) + dot_nt(d_up, wu_ref[j])
     d_log = (d_log - probs * inner).astype(BF)
-    dlog_ref[...] = d_log
-    dx += dot_nt(d_log, router_ref[...])
+    rest = jnp.zeros((n.shape[0], pack_ref.shape[1] - 2 * share - names), BF)
+    d_products = jnp.concatenate([d_gate_s, d_up_s, d_log, rest], -1)
+    dx += dot_nt(d_products, pack_ref[...])
+    dpack_ref[...] += dot_tn(n, d_products)
     out_ref[...] = out.astype(BF)
     dx_ref[...] = dx.astype(BF)
 
@@ -784,15 +860,14 @@
             move.finish()
 
 
-def experts(normed, cot, probs, weight, packed, eye, w_gate, w_up, w_down, s_gate, s_up, s_down, router):
+def experts(ranks, lanes, normed, cot, packed, w_gate, w_up, w_down, pack, s_down):
     total, width = normed.shape
     count, _, hidden = w_gate.shape
     tile = 256 if total % 256 == 0 else total
     steps = total // tile
+    share = s_down.shape[0]
     anywhere = pl.BlockSpec(memory_space=pl.ANY)
     dma = pltpu.SemaphoreType.DMA
-    names = probs.shape[1]
-    share = s_gate.shape[1]
 
     def rows(cols):
         return pl.BlockSpec((tile, cols), lambda i: (i, 0))
@@ -802,30 +877,26 @@
         return pl.BlockSpec(a.shape, lambda i: zeros, pipeline_mode=pl.Buffered(1))
 
     shape = jax.ShapeDtypeStruct
-    fixed = (eye, w_gate, w_up, w_down, s_gate, s_up, s_down, router)
+    fixed = (w_gate, w_up, w_down, pack, s_down)
     flops = total * width * hidden * count * 12
     return pl.pallas_call(
-        functools.partial(experts_kernel, count, steps),
+        functools.partial(experts_kernel, ranks, count, steps, share),
         grid=(steps,),
-        in_specs=[rows(width), rows(width), rows(names), rows(count)] + [whole(a) for a in fixed] + [anywhere] * 3,
+        in_specs=[rows(width), rows(width), rows(LANES)] + [whole(a) for a in fixed] + [anywhere] * 3,
         out_specs=[
             rows(width),
             rows(width),
-            rows(names),
-            pl.BlockSpec((width, share), lambda i: (0, 0)),
-            pl.BlockSpec((width, share), lambda i: (0, 0)),
+            pl.BlockSpec(pack.shape, lambda i: (0, 0)),
             pl.BlockSpec((share, width), lambda i: (0, 0)),
             anywhere, anywhere, anywhere,
         ],
         out_shape=[
             shape((total, width), BF),
             shape((total, width), BF),
-            shape((total, names), BF),
-            shape((width, share), F32),
-            shape((width, share), F32),
+            shape(pack.shape, F32),
             shape((share, width), F32),
             shape((6, total // 2, width), BF),
-            shape((6, total // 2, width // 2), BF),
+            shape((6, total // 2, lanes), BF),
             shape((6, total // 2, LANES), BF),
         ],
         scratch_shapes=[dma((3, Across.SEMAPHORES)), dma((3, Across.SEMAPHORES))],
@@ -834,15 +905,12 @@
         ),
         cost_estimate=pl.CostEstimate(flops=flops, bytes_accessed=30 * 2**20, transcendentals=0),
         name="experts",
-    )(normed, cot, probs, weight, *fixed, normed, cot, packed)
-
-
-def routed_tile(j, count, n, c1, c2, packed, w_gate, w_up, w_down, acc_gate, acc_up, acc_down):
-    part = c1.shape[-1]
+    )(normed, cot, packed, *fixed, normed, cot, packed)
+
+
+def routed_tile(j, count, n, c, packed, w_gate, w_up, w_down, acc_gate, acc_up, acc_down):
     weight = packed[:, j : j + 1].astype(F32) + packed[:, count + j : count + j + 1].astype(F32)
-    d_y = jnp.concatenate(
-        [(weight * c1.astype(F32)).astype(BF), (weight * c2.astype(F32)).astype(BF)], -1
-    )
+    d_y = jnp.concatenate([(weight * part.astype(F32)).astype(BF) for part in c], -1)
     gate, up = dot(n, w_gate), dot(n, w_up)
     d_gate, d_up = swiglu_back(dot_nt(d_y, w_down), gate, up)
     hidden = (silu(gate) * up).astype(BF)
@@ -852,7 +920,7 @@
 
 
 def weights_kernel(
-    j, count, first, size, own_steps, n_own, c_own, packed_own, n_ref, c1_ref, c2_ref, packed_ref,
+    j, count, first, size, own_steps, n_own, c_own, packed_own, n_ref, ca_ref, cb_ref, cc_ref, packed_ref,
     wg_ref, wu_ref, wd_ref, *refs,
 ):
     dg_ref, du_ref, dd_ref, wg, wu, wd, acc_gate, acc_up, acc_down, load, store = refs[-11:]
@@ -874,12 +942,15 @@
             copy.wait()
 
     ours = step < own_steps
-    part = c1_ref.shape[-1]
+    parts, at = [], 0
+    for ref in (ca_ref, cb_ref, cc_ref):
+        lanes = ref.shape[-1]
+        parts.append(jnp.where(ours, c_own[:, at : at + lanes], ref[0]))
+        at += lanes
     routed_tile(
         j, count,
         jnp.where(ours, n_own[...], n_ref[0]),
-        jnp.where(ours, c_own[:, :part], c1_ref[0]),
-        jnp.where(ours, c_own[:, part : 2 * part], c2_ref[0]),
+        parts,
         jnp.where(ours, packed_own[...], packed_ref[0]),
         wg[...], wu[...], wd[...], acc_gate, acc_up, acc_down,
     )
@@ -930,13 +1001,375 @@
             pltpu.VMEM((width, size), F32), pltpu.VMEM((width, size), F32), pltpu.VMEM((size, width), F32),
             dma((3,)), dma((3,)),
         ],
-        input_output_aliases={} if grads is None else {10: 0, 11: 1, 12: 2},
+        input_output_aliases={} if grads is None else {11: 0, 12: 1, 13: 2},
         compiler_params=pltpu.CompilerParams(vmem_limit_bytes=VMEM_LIMIT),
         cost_estimate=pl.CostEstimate(
             flops=slots * half * width * size * 12, bytes_accessed=40 * 2**20, transcendentals=0
         ),
         name="expert_weights",
     )(*own, *others, *weights, *before)
+
+
+class Scatter:
+    def __init__(self, part, pair, far, stage, mine, theirs, sems):
+        self.me = lax.axis_index("expert")
+        self.chips = part.shape[0]
+        self.z, self.c = self.me // 2, lax.rem(self.me, 2)
+        self.part, self.pair, self.far = part, pair, far
+        self.stage, self.mine, self.theirs = stage, mine, theirs
+        self.send, self.recv, self.local = sems
+        self.near = mine is None
+
+    def swap(self):
+        twin = self.me + 1 - 2 * self.c
+        return remote(self.part.at[:, 1 - self.c], self.pair, self.send.at[0], self.recv.at[0], expert=twin)
+
+    def own(self):
+        return pltpu.make_async_copy(self.part.at[:, self.c], self.stage, self.local.at[0])
+
+    def start(self):
+        self.swap().start()
+        if self.near:
+            self.own().start()
+
+    def hop(self, d):
+        to, source = lax.rem(self.z + d, self.chips), lax.rem(self.z + self.chips - d, self.chips)
+        out = remote(
+            self.stage.at[to], self.far.at[self.z], self.send.at[d], self.recv.at[d], expert=2 * to + self.c
+        )
+        back = remote(
+            self.stage.at[to], self.far.at[source], self.send.at[d], self.recv.at[d], expert=2 * to + self.c
+        )
+        return out, back
+
+    def load(self, src, dst, k):
+        copy = pltpu.make_async_copy(src, dst, self.local.at[k])
+        copy.start()
+        return copy
+
+    def add_pairs(self):
+        if self.near:
+            self.own().wait()
+        self.swap().wait_recv()
+
+        def one(i, carry):
+            if self.near:
+                self.stage[i] = (self.stage[i].astype(F32) + self.pair[i].astype(F32)).astype(BF)
+                return carry
+            copies = [self.load(self.part.at[i, self.c], self.mine, 0), self.load(self.pair.at[i], self.theirs, 1)]
+            for copy in copies:
+                copy.wait()
+            self.stage[i] = (self.mine[...].astype(F32) + self.theirs[...].astype(F32)).astype(BF)
+            return carry
+
+        lax.fori_loop(0, self.chips, one, 0)
+        for d in range(1, self.chips):
+            self.hop(d)[0].start()
+
+    def total(self):
+        acc = self.stage[self.z].astype(F32)
+        for d in range(1, self.chips):
+            self.hop(d)[1].wait_recv()
+            source = lax.rem(self.z + self.chips - d, self.chips)
+            if self.near:
+                acc += self.far[source].astype(F32)
+            else:
+                self.load(self.far.at[source], self.mine, 0).wait()
+                acc += self.mine[...].astype(F32)
+        return acc
+
+    def finish(self):
+        self.swap().wait_send()
+        for d in range(1, self.chips):
+            self.hop(d)[0].wait_send()
+
+
+def tail_kernel(
+    ranks, groups, heads, slots, j, count,
+    dn_ref, dwq_ref, dwk_ref, dwv_ref, dpack_ref,
+    n_own, c_own, packed_own, n_all, ca_all, cb_all, cc_all, packed_all, wg_ref, wu_ref, wd_ref,
+    dn_sum, all_ref, dg_ref, du_ref, dd_ref, *refs,
+):
+    if dn_ref.shape[0] > 4:
+        pair, far, mine, theirs = refs[:2] + refs[-2:]
+        refs = refs[2:-2]
+    else:
+        pair, far = refs[-2:]
+        mine = theirs = None
+        refs = refs[:-2]
+    (
+        n_buf, c_buf, p_buf, wg, wu, wd, acc_gate, acc_up, acc_down, got_ref, sum_ref, stage,
+        a_send, a_recv, a_local, r_send, r_recv, t_send, t_recv, g_send, g_recv,
+        e_send, e_recv, load, fetched,
+    ) = refs
+    me, g = lax.axis_index("expert"), lax.axis_index("dp")
+    width = n_own.shape[1]
+    rows = width // ranks
+    tile = n_buf.shape[1]
+    half = n_all.shape[1]
+    per = half // tile
+    own_steps = 2 * per
+    steps = own_steps + n_all.shape[0] * per
+    parts, at = [], 0
+    for ref in (ca_all, cb_all, cc_all):
+        parts.append(pl.ds(at, ref.shape[-1]))
+        at += ref.shape[-1]
+    peers = [lax.rem(g + d, groups) for d in range(1, groups)]
+    others = [lax.rem(me + d, ranks) for d in range(1, ranks)]
+    banks = (dwq_ref, dwk_ref, dwv_ref, dpack_ref)
+
+    meet([{"expert": t} for t in others] + [{"dp": t} for t in peers])
+    first = Scatter(dn_ref, pair, far, stage, mine, theirs, (a_send, a_recv, a_local))
+    first.start()
+
+    def slot(s):
+        return slice(s * LANES, (s + 1) * LANES)
+
+    def has(s, i, group):
+        return jnp.logical_or(group == groups - 1, head_of(s, i, ranks) < heads)
+
+    def reduce_copy(d, s, which):
+        return remote(
+            banks[which].at[:, slot(s)], got_ref.at[d - 1, :, slot(s)], r_send.at[d, s], r_recv.at[d, s], dp=peers[d - 1]
+        )
+
+    for d in range(1, groups):
+        for s in range(slots):
+            for which in range(groups):
+                ok = jnp.logical_and(peers[d - 1] == which, has(s, me, which))
+                pl.when(ok)(lambda: reduce_copy(d, s, which).start())
+
+    def fetch(t, into):
+        def ours():
+            r = aligned(t, tile)
+            return n_own.at[r], packed_own.at[r], *(c_own.at[r, part] for part in parts)
+
+        def theirs_():
+            k = t - own_steps
+            r = aligned(lax.rem(k, per), tile)
+            return tuple(ref.at[k // per, r] for ref in (n_all, packed_all, ca_all, cb_all, cc_all))
+
+        def go(sources):
+            for k, copy in enumerate(tile_copies(sources, into)):
+                copy.start()
+
+        pl.when(t < own_steps)(lambda: go(ours()))
+        pl.when(t >= own_steps)(lambda: go(theirs_()))
+
+    def tile_copies(sources, into):
+        targets = (n_buf.at[into], p_buf.at[into], *(c_buf.at[into, :, part] for part in parts))
+        return [
+            pltpu.make_async_copy(src, dst, fetched.at[into, k]) for k, (src, dst) in enumerate(zip(sources, targets))
+        ]
+
+    fetch(0, 0)
+    copies = [
+        pltpu.make_async_copy(wg_ref.at[j], wg, load.at[0]),
+        pltpu.make_async_copy(wu_ref.at[j], wu, load.at[1]),
+        pltpu.make_async_copy(wd_ref.at[j], wd, load.at[2]),
+    ]
+    for copy in copies:
+        copy.start()
+    for acc in (acc_gate, acc_up, acc_down):
+        acc[...] = jnp.zeros_like(acc)
+    for copy in copies:
+        copy.wait()
+
+    def turn_copy(d, s, i, to):
+        return remote(
+            sum_ref.at[to, :, slot(s)], all_ref.at[g, i, :, slot(s)], t_send.at[d, s], t_recv.at[d, s], expert=to
+        )
+
+    def add_groups():
+        for s in range(slots):
+            def one(s=s):
+                for d in range(1, groups):
+                    reduce_copy(d, s, 0).wait_recv()
+                for which in range(groups):
+                    def add(which=which):
+                        for r in range(ranks):
+                            here = slice(r * rows, (r + 1) * rows)
+                            acc = banks[which][here, slot(s)].astype(F32)
+                            for d in range(1, groups):
+                                acc += got_ref[d - 1, here, slot(s)].astype(F32)
+                            sum_ref[r, :, slot(s)] = acc.astype(BF)
+
+                    pl.when(g == which)(add)
+                all_ref[g, me, :, slot(s)] = sum_ref[me, :, slot(s)]
+                for d in range(1, ranks):
+                    turn_copy(d, s, me, others[d - 1]).start()
+
+            pl.when(has(s, me, g))(one)
+
+    def spread(d, s, group, to):
+        if (s + 1) * ranks <= heads:
+            part = all_ref.at[group, :, :, slot(s)]
+            return [(True, remote(part, part, g_send.at[d, s], g_recv.at[d, s], dp=to))]
+        whole = all_ref.at[group, :, :, slot(s)]
+        found = [(group == groups - 1, remote(whole, whole, g_send.at[d, s], g_recv.at[d, s], dp=to))]
+        for k, i in enumerate(i for i in range(ranks) if head_of(s, i, ranks) < heads):
+            part = all_ref.at[group, i, :, slot(s)]
+            found.append((group != groups - 1, remote(part, part, e_send.at[d, k], e_recv.at[d, k], dp=to)))
+        return found
+
+    def spread_out():
+        for d in range(1, ranks):
+            i = lax.rem(me + ranks - d, ranks)
+            for s in range(slots):
+                pl.when(has(s, i, g))(lambda: turn_copy(d, s, i, others[0]).wait_recv())
+        for d in range(1, groups):
+            for s in range(slots):
+                for ok, copy in spread(d, s, g, peers[d - 1]):
+                    guarded(ok, copy.start)
+
+    def keep_first():
+        dn_sum[...] = first.total()
+
+    hooks = [None, first.add_pairs, None, add_groups, None, spread_out, None, keep_first]
+
+    def step(t, carry):
+        now = lax.rem(t, 2)
+        pl.when(t + 1 < steps)(lambda: fetch(t + 1, 1 - now))
+        r = pl.ds(0, tile)
+        for copy in tile_copies((n_own.at[r], packed_own.at[r], *(c_own.at[r, part] for part in parts)), now):
+            copy.wait()
+        routed_tile(
+            j, count, n_buf[now], [c_buf[now]], p_buf[now],
+            wg[...], wu[...], wd[...], acc_gate, acc_up, acc_down,
+        )
+        for k, hook in enumerate(hooks):
+            if hook is not None:
+                pl.when(t == k * steps // len(hooks))(hook)
+        return carry
+
+    lax.fori_loop(0, steps, step, 0)
+    stores = [
+        pltpu.make_async_copy(acc_gate, dg_ref, load.at[0]),
+        pltpu.make_async_copy(acc_up, du_ref, load.at[1]),
+        pltpu.make_async_copy(acc_down, dd_ref, load.at[2]),
+    ]
+    for copy in stores:
+        copy.start()
+    first.finish()
+    for d in range(1, groups):
+        source = lax.rem(g + groups - d, groups)
+        for s in range(slots):
+            pl.when(has(s, me, peers[d - 1]))(lambda: reduce_copy(d, s, 0).wait_send())
+            for ok, copy in spread(d, s, source, peers[d - 1]):
+                guarded(ok, copy.wait_recv)
+            for ok, copy in spread(d, s, g, peers[d - 1]):
+                guarded(ok, copy.wait_send)
+    for d in range(1, ranks):
+        for s in range(slots):
+            pl.when(has(s, me, g))(lambda: turn_copy(d, s, me, others[d - 1]).wait_send())
+    for copy in stores:
+        copy.wait()
+
+
+def tail(ranks, groups, heads, slots, j, d_normed, d_weights, tokens, weights):
+    own_tokens, others = tokens
+    half, width = others[0].shape[1:]
+    count, _, hidden = weights[0].shape
+    chips = ranks // 2
+    total = d_normed.shape[0]
+    own = total // ranks
+    rows = width // ranks
+    span = slots * LANES
+    tile = min(512, half)
+    dma = pltpu.SemaphoreType.DMA
+    shape = jax.ShapeDtypeStruct
+    vmem, anywhere = pl.BlockSpec(memory_space=pltpu.VMEM), pl.BlockSpec(memory_space=pl.ANY)
+    block = shape((chips, own, width), BF)
+    near = chips <= 4
+    return pl.pallas_call(
+        functools.partial(tail_kernel, ranks, groups, heads, slots, j, count),
+        out_shape=[
+            shape((own, width), F32), shape((groups, ranks, rows, span), BF),
+            shape((width, hidden), F32), shape((width, hidden), F32), shape((hidden, width), F32),
+        ]
+        + [block] * (0 if near else 2),
+        in_specs=[anywhere] + [vmem] * 4 + [anywhere] * 11,
+        out_specs=[vmem] * 2 + [anywhere] * (3 if near else 5),
+        scratch_shapes=[
+            pltpu.VMEM((2, tile, width), BF), pltpu.VMEM((2, tile, width), BF), pltpu.VMEM((2, tile, LANES), BF),
+            pltpu.VMEM((width, hidden), BF), pltpu.VMEM((width, hidden), BF), pltpu.VMEM((hidden, width), BF),
+            pltpu.VMEM((width, hidden), F32), pltpu.VMEM((width, hidden), F32), pltpu.VMEM((hidden, width), F32),
+            pltpu.VMEM((groups - 1, width, span), BF), pltpu.VMEM((ranks, rows, span), BF),
+            pltpu.VMEM((chips, own, width), BF),
+            dma((chips,)), dma((chips,)), dma((2,)),
+            dma((groups, slots)), dma((groups, slots)),
+            dma((ranks, slots)), dma((ranks, slots)),
+            dma((groups, slots)), dma((groups, slots)),
+            dma((groups, ranks)), dma((groups, ranks)),
+            dma((3,)), dma((2, 5)),
+        ]
+        + ([pltpu.VMEM((chips, own, width), BF)] * 2 if near else [pltpu.VMEM((own, width), BF)] * 2),
+        compiler_params=pltpu.CompilerParams(
+            vmem_limit_bytes=VMEM_LIMIT, collective_id=4, has_side_effects=True
+        ),
+        cost_estimate=pl.CostEstimate(flops=total * groups * width * hidden * 12, bytes_accessed=2**26, transcendentals=0),
+        name="tail",
+    )(
+        d_normed.reshape(chips, 2, own, width), *d_weights,
+        *own_tokens, *others, *weights,
+    )[:5]
+
+
+def outputs_kernel(
+    heads, slots, j, gain_at, dn_ref, out_ref, resid_ref, dres_ref, x_ref, gain_ref, all_ref, wo_ref, sd_ref,
+    eg_ref, eu_ref, ed_ref, bg_ref, bu_ref, bd_ref,
+    layer_ref, dx_ref, q_ref, k_ref, v_ref, o_ref, sg_ref, su_ref, dsd_ref, small_ref, dg_ref, du_ref, dd_ref, store,
+):
+    copies = [
+        pltpu.make_async_copy(src, dst.at[j], store.at[k])
+        for k, (src, dst) in enumerate(((eg_ref, dg_ref), (eu_ref, du_ref), (ed_ref, dd_ref)))
+    ]
+    for copy in copies:
+        copy.start()
+    layer_ref[...] = (resid_ref[...] + out_ref[...].astype(F32)).astype(BF)
+    x = x_ref[...].astype(F32)
+    inverse = lax.rsqrt(jnp.mean(x * x, -1, keepdims=True) + EPS)
+    dx_ref[...] = (dres_ref[...] + norm_back(dn_ref[...], x, inverse, gain_ref[gain_at : gain_at + 1, :])).astype(BF)
+    ranks = all_ref.shape[1]
+    share = sg_ref.shape[1] // ranks
+    for which, ref in enumerate((q_ref, k_ref, v_ref)):
+        for h in range(heads):
+            s, i = next((s, i) for s in range(slots) for i in range(ranks) if head_of(s, i, ranks) == h)
+            ref[:, h * LANES : (h + 1) * LANES] = all_ref[which, i, :, s * LANES : (s + 1) * LANES].astype(F32)
+    last = all_ref.shape[0] - 1
+    small = jnp.zeros(small_ref.shape, F32)
+    for i in range(ranks):
+        here = all_ref[last, i].astype(F32)
+        sg_ref[:, i * share : (i + 1) * share] = here[:, :share]
+        su_ref[:, i * share : (i + 1) * share] = here[:, share : 2 * share]
+        small += here
+    small_ref[...] = small
+    o_ref[...] = wo_ref[...].astype(F32)
+    dsd_ref[...] = sd_ref[...].astype(F32)
+    for copy in copies:
+        copy.wait()
+
+
+def outputs(heads, slots, j, gain_at, share_width, arrays, last_grads, grads):
+    dn, out, resid, d_resid, x, gain, everything, d_wo, d_sd = arrays
+    rows, span = everything.shape[2:]
+    own, width = x.shape
+    shape = jax.ShapeDtypeStruct
+    vmem, anywhere = pl.BlockSpec(memory_space=pltpu.VMEM), pl.BlockSpec(memory_space=pl.ANY)
+    return pl.pallas_call(
+        functools.partial(outputs_kernel, heads, slots, j, gain_at),
+        out_shape=[shape((own, width), BF)] * 2
+        + [shape((rows, width), F32)] * 4
+        + [shape((rows, share_width), F32)] * 2
+        + [shape(d_sd.shape, F32), shape((rows, span), F32)]
+        + [shape(a.shape, F32) for a in grads],
+        in_specs=[vmem] * 12 + [anywhere] * 3,
+        out_specs=[vmem] * 10 + [anywhere] * 3,
+        scratch_shapes=[pltpu.SemaphoreType.DMA((3,))],
+        input_output_aliases={12: 10, 13: 11, 14: 12},
+        compiler_params=pltpu.CompilerParams(vmem_limit_bytes=VMEM_LIMIT),
+        name="outputs",
+    )(*arrays, *last_grads, *grads)
 
 
 def norm_back(grad, values, inverse, gain):
@@ -985,21 +1418,7 @@
         edges.append(edges[-1] + p.shape[-1])
     pack = jnp.concatenate(pieces, -1)
     pack = jnp.pad(pack, ((0, 0), (0, 0), (0, span - edges[-1])))
-    group_x, w_slices = front(
-        ranks, groups, heads, slots, tokens.reshape(own, width), w_query, w_key, w_value, pack
-    )
-    landed = w_slices[3]
-    s_gate = landed[:, edges[0] : edges[1]]
-    s_up = landed[:, edges[1] : edges[2]]
-    full_router = landed[:, edges[2] : edges[3]]
-    gain_one = landed[:, edges[3]][None, :]
-    gain_two = landed[:, edges[4]][None, :].astype(F32)
-    cosine, sine = rotary_tables(length)
-    inverse_one, q, k, v, mixed, lse, half_out = attend(
-        ranks, groups, seqs, slots, in_order(group_x), gain_one, w_slices[0], w_slices[1], w_slices[2],
-        cosine, sine, w_output,
-    )
-
+    gain_at = edges[3] - (slots - 1) * LANES
     top = expert_ids.shape[-1]
     extended = jnp.concatenate(
         [
@@ -1009,32 +1428,26 @@
         ],
         -1,
     )
-    group_c = lax.all_gather(extended, "expert", axis=0, tiled=True)
-    group_ids = group_c[:, width : width + top].astype(jnp.int32)
-
-    inputs = tokens.reshape(own, width).astype(F32)
-    resid, normed_two, all_mixed, all_out, all_c1 = project(
-        ranks, heads, slots, group_x, by_rank(mixed), half_out, gain_two, group_c
+    group_x, group_c, w_q, w_k, w_v, w_pack, small, half_out = front(
+        ranks, groups, heads, slots, tokens.reshape(own, width), extended, w_query, w_key, w_value, pack, w_output
     )
-    padded_out = jnp.pad(all_out, ((0, slots * ranks * HEAD_DIM - width), (0, 0)))
-    w_out = lax.dynamic_index_in_dim(
-        padded_out.reshape(slots, ranks, HEAD_DIM, width), me, 1, keepdims=False
-    ).reshape(span, width)
-
-    probs = jax.nn.softmax(dot(normed_two, full_router), axis=-1)
-    mine = me * count + jnp.arange(count)
-    chosen = jnp.any(group_ids[:, :, None] == mine[None, None, :], axis=1).astype(F32)
-    weight = chosen * lax.dynamic_slice_in_dim(probs, me * count, count, 1)
-    high = weight.astype(BF)
-    low = (weight - high.astype(F32)).astype(BF)
-    packed = jnp.concatenate([high, low, jnp.zeros((total, LANES - 2 * count), BF)], -1)
-    eye = (jnp.arange(names)[None, :] == mine[:, None]).astype(F32)
-    layer_part, d_normed_part, d_log, d_s_gate, d_s_up, d_s_down, all_n, all_c2, all_w = experts(
-        normed_two, group_c, probs, weight, packed, eye, expert_gate, expert_up, expert_down,
-        s_gate, s_up, shared_down, full_router,
+    group_c = group_c.reshape(total, -1)
+    gain_two = small[gain_at + 1 : gain_at + 2]
+    cosine, sine = rotary_tables(length)
+    units = width // LANES
+    c_first, c_last = max(units // 5, 1) * LANES, max(3 * units // 10, 1) * LANES
+    c_middle = width - c_first - c_last
+    inverse_one, q, k, v, mixed, lse, all_ca = attend(
+        seqs, slots, gain_at, c_first, in_order(group_x), small, w_q, w_k, w_v, cosine, sine, group_c
     )
-    router_part = dot_tn(normed_two, d_log)
-    every = ((normed_two, group_c, packed), (all_n, all_c1, all_c2, all_w))
+
+    resid, normed_two, all_mixed, all_out, packed, all_cb = project(
+        ranks, groups, heads, slots, count, top, edges[2], c_first, c_middle, group_x, by_rank(mixed), half_out, small, w_pack, group_c
+    )
+    layer_part, d_normed_part, d_pack, d_s_down, all_n, all_cc, all_w = experts(
+        ranks, c_last, normed_two, group_c, packed, expert_gate, expert_up, expert_down, w_pack, shared_down
+    )
+    every = ((normed_two, group_c, packed), (all_n, all_ca, all_cb, all_cc, all_w))
     banks = (expert_gate, expert_up, expert_down)
     hidden = expert_gate.shape[-1]
     cut = hidden * 4 // 7 if hidden % (7 * LANES) == 0 else hidden // 2
@@ -1058,62 +1471,28 @@
     d_att, grads = lax.optimization_barrier((d_att, grads))
 
     d_normed_part, d_wq, d_wk, d_wv, attn_gain_part = attend_back(
-        seqs, slots, in_order(d_att), in_order(group_x), inverse_one, gain_one, w_slices[:3], w_out,
-        cosine, sine, q, k, v, lse
+        ranks, heads, seqs, slots, gain_at, in_order(d_att), in_order(group_x), inverse_one, small,
+        (w_q, w_k, w_v), all_out, cosine, sine, q, k, v, lse
     )
-    d_qkv = jnp.concatenate([d_wq, d_wk, d_wv], -1)
-    grads = expert_weights(1, 0, hidden, after(every, attn_gain_part), banks, grads)
-    g_gate, g_up, g_down = grads
-    d_normed_one = scatter(by_rank(d_normed_part)).astype(F32)
-    own_inverse = lax.rsqrt(jnp.mean(inputs * inputs, -1, keepdims=True) + EPS)
-    input_grad = d_resid + norm_back(d_normed_one, inputs, own_inverse, gain_one.astype(F32))
-    layer_output = resid + scatter(layer_part).astype(F32)
+    column = jnp.arange(span)[None, :]
+    d_pack = jnp.where(column == edges[3], attn_gain_part.reshape(width, 1), d_pack)
+    d_pack = jnp.where(column == edges[4], ffn_gain_part[:, None], d_pack).astype(BF)
     own_mixed = lax.dynamic_slice_in_dim(all_mixed, me * rows, rows, 1)
     d_wo_rows = dot_tn(own_mixed, d_att).astype(BF)
-
-    def to_rows(g):
-        return g.reshape(ranks, rows, -1)
-
-    pieces = [
-        to_rows(d_qkv), to_rows(d_s_gate.astype(BF)), to_rows(d_s_up.astype(BF)), to_rows(router_part.astype(BF)),
-        to_rows(attn_gain_part.astype(BF)), to_rows(ffn_gain_part.astype(BF)),
-    ]
-    used = sum(p.shape[-1] for p in pieces)
-    packed = jnp.pad(jnp.concatenate(pieces, -1), ((0, 0), (0, 0), (0, -used % LANES)))
-    landed = lax.all_to_all(packed, "expert", 0, 0, tiled=True)
-    edges = [0]
-    for p in pieces:
-        edges.append(edges[-1] + p.shape[-1])
-
-    def heads_back(part):
-        part = part.reshape(ranks, rows, slots, HEAD_DIM).transpose(1, 2, 0, 3)
-        return part.reshape(rows, slots * ranks * HEAD_DIM)[:, :width]
-
-    def shares_back(part):
-        return part.transpose(1, 0, 2).reshape(rows, ranks * share)
-
-    def summed(part):
-        return jnp.sum(part.astype(F32), 0).astype(BF)
-
-    sums = lax.psum(
-        (
-            heads_back(landed[:, :, :span]),
-            heads_back(landed[:, :, span : 2 * span]),
-            heads_back(landed[:, :, 2 * span : 3 * span]),
-            d_wo_rows,
-            shares_back(landed[:, :, edges[1] : edges[2]]),
-            shares_back(landed[:, :, edges[2] : edges[3]]),
-            summed(landed[:, :, edges[3] : edges[4]]),
-            summed(landed[:, :, edges[4]]),
-            summed(landed[:, :, edges[5]]),
-            d_s_down.astype(BF),
-        ),
-        "dp",
+    d_wo_rows, d_sd_rows = lax.psum((d_wo_rows, d_s_down.astype(BF)), "dp")
+    dn_sum, all_grads, *last_grads = tail(
+        ranks, groups, heads, slots, 1, by_rank(d_normed_part), (d_wq, d_wk, d_wv, d_pack), every, banks
     )
-    g_q, g_k, g_v, g_o, g_sg, g_su, g_r, g_one, g_two, g_sd = [s.astype(F32) for s in sums]
+    layer_output, input_grad, g_q, g_k, g_v, g_o, g_sg, g_su, g_sd, small, g_gate, g_up, g_down = outputs(
+        heads, slots, 1, gain_at, ranks * share,
+        (dn_sum, scatter(after(layer_part, d_att)), resid, d_resid, tokens.reshape(own, width), small, all_grads, d_wo_rows, d_sd_rows),
+        last_grads, grads,
+    )
+    g_r = small[:, edges[2] : edges[3]]
+    g_one = small[:, edges[3]]
+    g_two = small[:, edges[4]]
     return (
-        layer_output.astype(BF).reshape(tokens.shape),
-        input_grad.astype(BF).reshape(tokens.shape),
+        layer_output.reshape(tokens.shape), input_grad.reshape(tokens.shape),
         g_one, g_two, g_q, g_k, g_v, g_o, g_r, g_sg, g_su, g_sd, g_gate, g_up, g_down,
     )
 

time: 674 us -> 504 us (0.75)
  the two profiles are of different devices: /device:TPU:0 before, /device:TPU:13 now
where the time goes in v2:
time: 504 us; the launch traced here: 499 us
  Pallas kernels  457 us (91%)
  between operations  14.5 us (3%)
  local copies, waits for them, and re-layouts  13.8 us (3%)
  other arithmetic  9.47 us (2%)
    pallas_call x1, Pallas kernels, tail(): pl.pallas_call(functools.partial(tail_kernel, ranks, groups, heads, slots...  124 us
    pallas_call x2, Pallas kernels, expert_weights(): pl.pallas_call(functools.partial(weights_kernel, j, count, first, size, o...  82.5 us
    pallas_call x1, Pallas kernels, experts(): pl.pallas_call(functools.partial(experts_kernel, ranks, count, steps, sha...  80.1 us
    pallas_call x1, Pallas kernels, front(): pl.pallas_call(functools.partial(front_kernel, ranks, groups, heads, slot...  70.9 us
    pallas_call x1, Pallas kernels, project(): pl.pallas_call(functools.partial(project_kernel, ranks, groups, heads, sl...  44.1 us
    pallas_call x1, Pallas kernels, attend(): pl.pallas_call(functools.partial(attend_kernel, seqs, slots, gain_at), ou...  22.9 us
    pallas_call x1, Pallas kernels, vmem_call(): pl.pallas_call(kernel, out_shape=outs, in_specs=[spec] * len(args), out_s...  18.3 us
    pallas_call x1, Pallas kernels, outputs(): pl.pallas_call(functools.partial(outputs_kernel, heads, slots, j, gain_at...  14.4 us
  transfers between devices with their start and end apart: 4, of which 0 were waited for; matrix products, arithmetic and copies ran while one was open for 1% of the time, Pallas kernels for 45%

profile of v2, /device:TPU:13, one launch (start us, length us, event | category | flops | bytes accessed | tf_op | source)
XLA Modules:
  0.0 499.3 jit_solution(3448562024597350394)
XLA Ops:
  7.2 0.0 copy-start.4
  7.2 0.0 copy-start.5
  7.2 0.0 reduce-scatter.3.cloned.1.call-start
  7.3 0.8 copy.43
  8.1 0.8 copy.40
  8.9 1.3 reshape.105
  10.2 1.3 reshape.106
  11.6 0.1 copy_bitcast_fusion
  11.7 0.0 copy-done.4
  11.7 0.0 copy-start.2
  11.7 0.1 broadcast_in_dim.55
  11.8 0.0 copy-done.5
  11.9 0.1 broadcast_in_dim.56
  12.0 3.0 concatenate.13
  14.9 1.0 pad.4.pack_ref
  15.9 1.9 fusion.8
  17.8 0.0 copy-done.2
  17.8 0.8 concatenate.12.c_ref
  18.7 1.3 pad_maximum_fusion
  20.0 70.9 %front.1 = (bf16[8,128,1280]{2,1,0:T(8,128)(2,1)}, bf16[8,128,1408]{2,1,0:T(8,128)(2,1)}, bf16[1280,256]{1,0:T(8,128)(2,1)}, bf16[1280,256]{1,0:T(8,128)(2,1)}, ...) custom-call(bf16[128,1280]{1,0:T(8,128)(2,1)} %bitcast.25, ...), custom_call_target="tpu_custom_call" | custom-call | tf_op jit(solution)/shard_map/front/pallas_call | solution.py:428
  90.9 22.9 %attend.1 = (f32[1024,1]{1,0:T(8,128)}, bf16[1024,256]{1,0:T(8,128)(2,1)}, bf16[1024,256]{1,0:T(8,128)(2,1)}, bf16[1024,256]{1,0:T(8,128)(2,1)}, bf16[1024,256]{...) custom-call(bf16[1024,1280]{1,0:T(8,128)(2,1)} %bitcast.16, ...), custom_call_target="tpu_custom_call" | custom-call | tf_op jit(solution)/shard_map/attend/pallas_call | solution.py:664
  113.8 44.1 %project.1 = (f32[128,1280]{1,0:T(8,128)}, bf16[1024,1280]{1,0:T(8,128)(2,1)}, bf16[1024,1280]{1,0:T(8,128)(2,1)}, bf16[1280,1280]{1,0:T(8,128)(2,1)}, bf16[1024...) custom-call(bf16[8,128,1280]{2,1,0:T(8,128)(2,1)} %get-tuple-element.89.x_ref, ...), custom_call_target="tpu_custom_call" | custom-call | tf_op jit(solution)/shard_map/project/pallas_call | solution.py:579
  157.8 80.1 %experts.1 = (bf16[1024,1280]{1,0:T(8,128)(2,1)}, bf16[1024,1280]{1,0:T(8,128)(2,1)}, f32[1280,256]{1,0:T(8,128)}, f32[112,1280]{1,0:T(8,128)}, bf16[6,512,1280]...) custom-call(bf16[1024,1280]{1,0:T(8,128)(2,1)} %get-tuple-element.111.n_ref.n_group.n_own, ...), custom_call_target="tpu_custom_call" | custom-call | flops 28185722880 | bytes 31457280 | tf_op jit(solution)/shard_map/experts/pallas_call | solution.py:882
  237.9 0.0 copy-start
  237.9 0.0 reduce-scatter.3.cloned.1.call-update
  238.0 0.0 all-gather.2.cloned.1.call-start
  238.0 0.9 slice_reduce_fusion.2
  238.9 0.2 copy-done
  239.0 0.1 multiply_reduce_fusion
  239.2 42.5 %expert_weights.2 = (f32[2,1280,896]{2,1,0:T(8,128)}, f32[2,1280,896]{2,1,0:T(8,128)}, f32[2,896,1280]{2,1,0:T(8,128)}) custom-call(bf16[1024,1280]{1,0:T(8,128)(2,1)} %get-tuple-element.111.n_ref.n_group.n_own, bf16[1024,1408]{1,0:T(8,128)(2,1)} %bitcast.22, bf16[1024,128]{1,0:T(8,128)(2,1)} %get-tuple-element.113.packed_ref.w_group.packed_own, ...), custom_call_target="tpu_custom_call" | custom-call | flops 24159191040 | bytes 41943040 | tf_op jit(solution)/shard_map/expert_weights/pallas_call | solution.py:992
  281.7 0.0 copy-start.3
  281.7 0.0 reduce-scatter.3.cloned.1.call-done
  281.7 1.3 fusion.6
  283.0 2.1 fusion.10
  285.1 0.0 all-gather.2.cloned.1.call-update
  285.1 0.0 all-reduce.4.cloned.1.call-start
  285.2 0.0 copy-done.3
  285.2 0.7 convert_element_type.47
  285.9 40.0 %expert_weights.3 = (f32[2,1280,896]{2,1,0:T(8,128)}, f32[2,1280,896]{2,1,0:T(8,128)}, f32[2,896,1280]{2,1,0:T(8,128)}) custom-call(bf16[1024,1280]{1,0:T(8,128)(2,1)} %get-tuple-element.111.n_ref.n_group.n_own, bf16[1024,1408]{1,0:T(8,128)(2,1)} %bitcast.23, ...), custom_call_target="tpu_custom_call", output_to_operand_aliasing={{0}: (11, {}), {1}: (12, {}), {2}: (13, {})} | custom-call | flops 18119393280 | bytes 41943040 | tf_op jit(solution)/shard_map/expert_weights/pallas_call | solution.py:992
  326.0 0.0 all-gather.2.cloned.1.call-done.da_ref
  326.0 3.5 convolution_convert_fusion
  329.5 0.0 all-reduce.4.cloned.1.call-update
  329.5 0.3 reduce-scatter.5.cloned.1.call-start
  329.8 0.3 reduce-scatter.5.cloned.1.call-update
  330.1 0.0 copy-start.1
  330.1 18.3 %attend_back.1 = (bf16[1024,1280]{1,0:T(8,128)(2,1)}, bf16[1280,256]{1,0:T(8,128)(2,1)}, bf16[1280,256]{1,0:T(8,128)(2,1)}, bf16[1280,256]{1,0:T(8,128)(2,1)}, f32[1,1280]{1,0:T(1,128)}) custom-call(bf16[1024,1280]{1,0:T(8,128)(2,1)} %all-gather.2.cloned.1.call-done.da_ref, bf16[1024,1280]{1,0:T(8,128)(2,1)} %bitcast.17, ...), custom_call_target="tpu_custom_call" | custom-call | tf_op jit(solution)/shard_map/attend_back/pallas_call | solution.py:53
  348.4 0.7 reduce.1
  349.1 0.0 copy-done.1
  349.1 1.2 select_convert_fusion.dpack_ref
  350.4 124.0 %tail.1 = (f32[128,1280]{1,0:T(8,128)}, bf16[4,8,160,256]{3,2,1,0:T(8,128)(2,1)}, f32[1280,896]{1,0:T(8,128)}, f32[1280,896]{1,0:T(8,128)}, f32[896,1280]{1,0:T(8,128)}) custom-call(bf16[4,2,128,1280]{3,2,1,0:T(8,128)(2,1)} %bitcast.28, bf16[1280,256]{1,0:T(8,128)(2,1)} %get-tuple-element.133.dwq_ref, bf16[1280,256]{1,0:T(8,128)(2,1)} %get-tuple-element.134.dwk_ref, ...), custom_call_target="tpu_custom_call" | custom-call | flops 56371445760 | bytes 67108864 | tf_op jit(solution)/shard_map/tail/pallas_call | solution.py:1284
  474.4 0.0 all-reduce.4.cloned.1.call-done
  474.4 0.0 reduce-scatter.5.cloned.1.call-done.out_ref
  474.4 14.4 %outputs.1 = (bf16[128,1280]{1,0:T(8,128)(2,1)}, bf16[128,1280]{1,0:T(8,128)(2,1)}, f32[160,1280]{1,0:T(8,128)}, f32[160,1280]{1,0:T(8,128)}, f32[160,1280]{1,0:...) custom-call(f32[128,1280]{1,0:T(8,128)} %get-tuple-element.138.dn_re, ...), custom_call_target="tpu_custom_call", output_to_operand_aliasing={{10}: (12, {}), {11}: (13, {}), {12}: (14, {})} | custom-call | tf_op jit(solution)/shard_map/outputs/pallas_call | solution.py:1359
  488.9 1.8 slice_reduce_fusion
  490.6 1.0 slice.15
  491.6 0.7 copy.44
  (8 shorter events, 0.1 us)
Async XLA Ops:
  7.2 4.5 copy-start.4
  7.2 4.7 copy-start.5
  7.2 274.5 %reduce-scatter.3.cloned.1.call-start = ((), (), s32[]{:S(2)}) async-start(), calls=%async_computation.2 | async-start | bytes 2949120 | tf_op jit(solution)/shard_map/reduce_scatter | solution.py:1459
  11.7 6.1 %copy-start.2 = (bf16[1,128,1280]{2,1,0:T(8,128)(2,1)S(1)}, bf16[1,128,1280]{2,1,0:T(8,128)(2,1)}, u32[]{:S(2)}) copy-start(bf16[1,128,1280]{2,1,0:T(8,128)(2,1)} %param.17) | copy-start | bytes 983044
  237.9 1.1 copy-start
  238.0 88.0 %all-gather.2.cloned.1.call-start = ((), (), s32[]{:S(2)}) async-start(), calls=%async_computation.3 | async-start | bytes 2949120 | tf_op jit(solution)/shard_map/all_gather | solution.py:1469
  281.7 3.5 copy-start.3
  285.1 189.3 %all-reduce.4.cloned.1.call-start = ((), (), s32[]{:S(2)}) async-start(), calls=%async_computation.5 | async-start | bytes 1392640 | tf_op jit(solution)/shard_map/psum | solution.py:1482
  329.5 144.9 %reduce-scatter.5.cloned.1.call-start = ((), (), s32[]{:S(2)}) async-start(), calls=%async_computation.4 | async-start | bytes 2949120 | tf_op jit(solution)/shard_map/reduce_scatter | solution.py:1459
  330.1 19.0 %copy-start.1 = (f32[1280,256]{1,0:T(8,128)S(1)}, f32[1280,256]{1,0:T(8,128)}, u32[]{:S(2)}) copy-start(f32[1280,256]{1,0:T(8,128)} %get-tuple-element.137) | copy-start | bytes 3932164
Sparse Core Ops, SparseCore 0:
  238.1 38.1 reduce-scatter.2
  285.3 38.8 all-gather.1
  329.6 67.2 all-reduce.3
  399.2 51.3 reduce-scatter.4
